TPU v7x, 256 devices: a whole 4x4x8 slice. The times are simulated.
256 devices in a mesh: axial: 16 (over x, y), pitch: 16 (over z, core).
Axes of the slice: x: 4, y: 4, z: 8, core: 2. Of those that a mesh axis runs over, the one named last changes fastest.
Arguments:
- adjoint_start: float32 [128, 35, 2048], P('axial', None, 'pitch'), may hold values from -6 to 6
- source: float32 [128, 35, 2048], P('axial', None, 'pitch'), may hold values from -0.07 to 0.07
- couple_block: float32 [128, 35, 35], P('axial'), may hold values from -0.05 to 2.9, as said below
- shift_diag: float32 [128, 35], P('axial'), may hold values from 0.0005 to 0.0015
- pitch_gain: float32 [128, 35], P('axial'), may hold values from 0.0003 to 0.001
- row_map: int32 [2048], replicated, may hold values from 0 to 2047, each once
- slide: int32 [7], replicated, may hold values from 0 to 2047
Outputs:
- adjoint_field: float32 [128, 35, 2048], P('axial', None, 'pitch')
Inputs may be any that keep to these rules, and one draw needn't show every extreme that they name: `row_map`: each line number appears once. `couple_block`: symmetric in its last two dimensions; each diagonal entry exceeds the sum of the magnitudes of the other entries of its row by 0.3 or more.
All inputs are finite; a program needn't handle non-finite values.
Results may differ from a plain program's by a relative error of at most 0.0003.
Values sent between devices are 32-bit elements; how exact they have to be, the bound alone decides.
A program may use at most 64 MiB of HBM per device.

v0:
```python
import jax
import jax.numpy as jnp
from jax import lax
from jax.sharding import PartitionSpec as P

VARS = 5
SWEEPS = 2


HIGHEST = lax.Precision.HIGHEST


def from_behind(block, axis, distance):
    devices = range(lax.axis_size(axis))
    route = [(i - distance, i) for i in devices if i - distance in devices]
    return lax.ppermute(block, axis, route)


def with_halo(x, sides, width, wrap):
    for axis, dim in sides:
        devices, length = (lax.axis_size(axis), x.shape[dim])
        up = [(i, (i + 1) % devices) for i in range(devices if wrap else devices - 1)]
        down = [(j, i) for i, j in up]
        last = lax.slice_in_dim(x, length - width, length, axis=dim)
        leading = lax.slice_in_dim(x, 0, width, axis=dim)
        before = lax.ppermute(last, axis, up)
        after = lax.ppermute(leading, axis, down)
        x = jnp.concatenate([before, x, after], axis=dim)
    return x


def product(left, right):
    return jnp.dot(left, right, precision=HIGHEST)


def inverse(matrix):
    factor = jnp.linalg.cholesky(matrix)
    return jax.scipy.linalg.cho_solve((factor, True), jnp.eye(matrix.shape[0], dtype=jnp.float32))


def solve_spd(matrix, right):
    return jax.scipy.linalg.cho_solve((jnp.linalg.cholesky(matrix), True), right)


def choose(flag, first, second):
    return jax.tree.map(lambda upper, lower: jnp.where(flag, upper, lower), first, second)


def join(left, right):
    left_flag, left_p, left_q, left_r, left_k, left_a, left_b = left
    right_flag, right_p, right_q, right_r, right_k, right_a, right_b = right
    width = left_p.shape[0]
    coupling = left_k * right_flag
    blank = jnp.zeros_like(left_p)
    middle = jnp.concatenate(
        [jnp.concatenate([left_r, coupling], 1), jnp.concatenate([coupling.T, right_p], 1)], 0
    )
    outer = jnp.concatenate(
        [jnp.concatenate([left_q.T, blank], 1), jnp.concatenate([blank, right_q], 1)], 0
    )
    factor = jnp.linalg.cholesky(middle)
    solved = jax.scipy.linalg.cho_solve((factor, True), outer)
    values = jax.scipy.linalg.cho_solve((factor, True), jnp.concatenate([left_b, right_a], 0))
    upper_part = product(left_q, solved[:width])
    first = left_p - upper_part[:, :width]
    cross = -upper_part[:, width:]
    last = right_r - product(right_q.T, solved[width:, width:])
    head = left_a - product(left_q, values[:width])
    tail = right_b - product(right_q.T, values[width:])
    joined = (jnp.maximum(left_flag, right_flag), first, cross, last, right_k, head, tail)
    keep_right = choose(left_flag[0] == 0.0, right, joined)
    return choose(right_flag[0] == 0.0, left, keep_right)


def boundary_forces(before, after, reduced_own, summary_rhs, own_link):
    width = own_link.shape[0]
    _, prior_p, prior_q, prior_r, prior_k, prior_a, prior_b = before
    _, later_p, later_q, later_r, _, later_a, later_b = after
    folded = product(prior_q.T, inverse(prior_p))
    left_inverse = inverse(prior_r - product(folded, prior_q))
    left_value = prior_b - product(folded, prior_a)
    bent = product(later_q, inverse(later_r))
    right_inverse = inverse(later_p - product(bent, later_q.T))
    right_value = later_a - product(bent, later_b)
    left_gain = product(prior_k.T, left_inverse)
    right_gain = product(own_link, right_inverse)
    blank = jnp.zeros_like(own_link)
    correction = jnp.concatenate(
        [
            jnp.concatenate([product(left_gain, prior_k), blank], 1),
            jnp.concatenate([blank, product(right_gain, own_link.T)], 1),
        ],
        0,
    )
    moved = jnp.concatenate([product(left_gain, left_value), product(right_gain, right_value)], 0)
    ends = solve_spd(reduced_own - correction, summary_rhs - moved)
    left_end = product(left_inverse, left_value - product(prior_k, ends[:width]))
    right_end = product(right_inverse, right_value - product(own_link.T, ends[width:]))
    return jnp.concatenate([product(prior_k.T, left_end), product(own_link, right_end)], 0)


def fold_upstream(stacked, identity, position, count):

    def step(carry, inputs):
        total, found = carry
        item, index = inputs
        found = choose(index == position, total, found)
        return ((join(total, item), found), None)

    (_, found), _ = lax.scan(
        step, (identity, identity), (stacked, jnp.arange(count, dtype=jnp.int32))
    )
    return found


def fold_downstream(stacked, identity, position, count):

    def step(carry, inputs):
        total, found = carry
        item, index = inputs
        found = choose(index == position, total, found)
        return ((join(item, total), found), None)

    (_, found), _ = lax.scan(
        step, (identity, identity), (stacked, jnp.arange(count, dtype=jnp.int32)), reverse=True
    )
    return found


def body(adjoint_start, source, couple_block, shift_diag, pitch_gain, row_map, slide):
    cells, width, lines = source.shape
    axial_count = lax.axis_size("axial")
    position = lax.axis_index("axial")
    line_start = lax.axis_index("pitch") * lines
    total_lines = lines * lax.axis_size("pitch")
    eye = jnp.eye(width, dtype=jnp.float32)
    last_link = from_behind(couple_block[-1], "axial", 1)
    before_link = jnp.concatenate([last_link[None], couple_block[:-1]], 0)
    at_cut = jnp.logical_or(position == axial_count // 2 - 1, position == axial_count - 1)
    outward = jnp.where(at_cut, 0.0, 1.0).astype(jnp.float32)
    diag_full = before_link + couple_block + (shift_diag + 2.0 * pitch_gain)[:, :, None] * eye

    def factor_step(current, inputs):
        diagonal, coupling = inputs
        inverted = inverse(current)
        forward = product(coupling, inverted)
        return (diagonal - product(forward, coupling), (inverted, forward))

    last_pivot, (inverses, forwards) = lax.scan(
        factor_step, diag_full[0], (diag_full[1:], couple_block[:-1])
    )
    inverses = jnp.concatenate([inverses, inverse(last_pivot)[None]], 0)
    backwards = jnp.swapaxes(forwards, 1, 2)

    def solve_line(right):

        def down(carry, inputs):
            row, forward = inputs
            return (row + product(forward, carry), carry)

        def up(carry, inputs):
            row, inverted, backward = inputs
            value = product(inverted, row) + product(backward, carry)
            return (value, value)

        last_row, rows = lax.scan(down, right[0], (right[1:], forwards))
        rows = jnp.concatenate([rows, last_row[None]], 0)
        last_value = product(inverses[-1], rows[-1])
        _, values = lax.scan(up, last_value, (rows[:-1], inverses[:-1], backwards), reverse=True)
        return jnp.concatenate([values, last_value[None]], 0)

    units = jnp.zeros((cells, width, 2 * width), jnp.float32)
    units = units.at[0, :, :width].set(eye).at[-1, :, width:].set(eye)
    responses = solve_line(units)
    reduced_own = inverse(jnp.concatenate([responses[0], responses[-1]], 0))
    own_link = -couple_block[-1] * outward
    zero_block = jnp.zeros((width, width), jnp.float32)
    zero_rows = jnp.zeros((width, lines), jnp.float32)
    identity = (
        jnp.zeros((1,), jnp.float32),
        eye,
        zero_block,
        eye,
        zero_block,
        zero_rows,
        zero_rows,
    )
    local_map = lax.dynamic_slice_in_dim(row_map, line_start, lines)
    lookup = (local_map[None, :] + jnp.repeat(slide, VARS)[:, None]) % total_lines
    field = adjoint_start
    for sweep in range(SWEEPS):
        padded = with_halo(field, (("axial", 0),), 1, False)
        widened = with_halo(field, (("pitch", 2),), 1, True)
        gathered = lax.all_gather(padded[0], "pitch", axis=1, tiled=True)
        mapped = jnp.take_along_axis(gathered, lookup, axis=1)
        lower_rim = jnp.where(position == axial_count // 2, mapped, padded[0])
        below = jnp.concatenate([lower_rim[None], field[:-1]], 0)
        above = jnp.concatenate([field[1:], padded[-1][None]], 0)
        applied = (
            jnp.einsum("lbc,lcm->lbm", diag_full, field, precision=HIGHEST)
            - jnp.einsum("lbc,lcm->lbm", before_link, below, precision=HIGHEST)
            - jnp.einsum("lbc,lcm->lbm", couple_block, above, precision=HIGHEST)
            - pitch_gain[:, :, None] * (widened[:, :, :-2] + widened[:, :, 2:])
        )
        residual = source - applied
        local_solution = solve_line(residual)
        summary_rhs = product(
            reduced_own, jnp.concatenate([local_solution[0], local_solution[-1]], 0)
        )
        element = (
            jnp.ones((1,), jnp.float32),
            reduced_own[:width, :width],
            reduced_own[:width, width:],
            reduced_own[width:, width:],
            own_link,
            summary_rhs[:width],
            summary_rhs[width:],
        )
        stacked = (
            lax.all_gather(element[0][None], "axial", axis=0, tiled=True),
            lax.all_gather(element[1][None], "axial", axis=0, tiled=True),
            lax.all_gather(element[2][None], "axial", axis=0, tiled=True),
            lax.all_gather(element[3][None], "axial", axis=0, tiled=True),
            lax.all_gather(element[4][None], "axial", axis=0, tiled=True),
            lax.all_gather(element[5][None], "axial", axis=0, tiled=True),
            lax.all_gather(element[6][None], "axial", axis=0, tiled=True),
        )
        before = fold_upstream(stacked, identity, position, axial_count)
        after = fold_downstream(stacked, identity, position, axial_count)
        forces = boundary_forces(before, after, reduced_own, summary_rhs, own_link)
        update = local_solution - jnp.einsum("lbc,cm->lbm", responses, forces, precision=HIGHEST)
        field = field + update
    return field


def solution(mesh):
    return jax.shard_map(
        body,
        mesh=mesh,
        in_specs=(
            P("axial", None, "pitch"),
            P("axial", None, "pitch"),
            P("axial", None, None),
            P("axial", None),
            P("axial", None),
            P(),
            P(),
        ),
        out_specs=P("axial", None, "pitch"),
        check_vma=False,
    )
```

profile of v0, /device:TPU:31, one launch (start us, length us, event | category | flops | bytes accessed | tf_op | source)
XLA Modules:
  0.0 2046.9 jit_solution(2126536793805703965)
XLA Ops:
  16.4 19.0 all_gather.43
  35.4 28.4 %all-reduce.13 = f32[16]{0:T(128)S(1)} all-reduce(f32[16]{0:T(128)S(1)} %dynamic-update-slice.10), channel_id=1, replica_groups=mesh['axial'=16,'pitch'=16] {'axial'}, use_global_device_ids=true, to_apply=%add.13 | all-reduce | flops 16 | bytes 128
  71.1 60.9 %while.240 = (s32[]{:T(128)}, f32[35,35]{1,0:T(8,128)S(1)}, f32[7,35,35]{2,1,0:T(8,128)}, f32[7,35,35]{2,1,0:T(8,128)S(1)}, f32[7,35,35]{2,1,0:T(8,128)S(1)}, /*index=5*/f32[7,35,35]{2,1,0:T(8,128)S(1)}, s32[]{:T(128)}) while((s32[]{:T(128)}, f32[35,35]{1,0:T(8,128)S(1)}, f32[7,35,35]{2,1,0:T(8,128)}, f32[7,35,35]{2,1,0:T(8,128)S(1)}, ...), condition=%wide.region_3.6_spmd, body=%wide.region_0.5_spmd.sunk | while | flops 2072736 | bytes 234859 | solution.py:149
  142.2 7.7 while.244
  150.4 6.4 cholesky.347
  164.8 18.2 all-gather.9
  183.2 18.8 all-gather.11
  202.3 15.6 all-gather.10
  217.9 48.1 %all-gather = f32[1,35,2048]{2,1,0:T(8,128)S(1)} all-gather(f32[1,35,128]{2,1,0:T(8,128)S(1)} %collective-permute-done.1), channel_id=2, replica_groups=mesh['axial'=16,'pitch'=16] {'pitch'}, dimensions={2}, use_global_device_ids=true | all-gather | bytes 304640 | tf_op jit(solution)/shard_map/all_gather | solution.py:194
  266.0 34.1 %gather_fusion = f32[4480]{0:T(1024)S(1)} fusion(f32[35,2048]{1,0:T(8,128)S(1)} %bitcast.964, s32[4480]{0:T(1024)S(1)} %fusion.351), kind=kCustom, calls=%fused_computation.clone | custom fusion | bytes 71680 | tf_op jit(solution)/shard_map/jit(take_along_axis)/gather | solution.py:195
  305.1 7.7 while.242
  313.7 20.3 all-gather.12
  334.0 18.3 all-gather.13
  352.3 435.4 %while.248 = (s32[]{:T(128)}, f32[1]{0:T(128)}, f32[35,35]{0,1:T(8,128)S(1)}, f32[35,35]{0,1:T(8,128)S(1)}, f32[35,35]{0,1:T(8,128)S(1)}, /*index=5*/f32[35,128]...) while((s32[]{:T(128)}, f32[1]{0:T(128)}, ...), condition=%wide.region_17.24_spmd.clone, body=%wide.region_16.23_spmd.clone.sunk | while | flops 28767804 | bytes 1750111 | solution.py:124
  358.1 6.4 cholesky.812
  385.4 6.4 cholesky.812
  412.7 6.4 cholesky.812
  440.0 6.4 cholesky.812
  467.3 6.4 cholesky.812
  494.6 6.4 cholesky.812
  521.9 6.4 cholesky.812
  549.2 6.4 cholesky.812
  576.5 6.4 cholesky.812
  603.9 6.4 cholesky.812
  631.2 6.4 cholesky.812
  658.5 6.4 cholesky.812
  685.8 6.4 cholesky.812
  713.1 6.4 cholesky.812
  740.4 6.4 cholesky.812
  767.7 6.4 cholesky.812
  807.4 353.2 %while.247 = (s32[]{:T(128)}, f32[1]{0:T(128)}, f32[35,35]{0,1:T(8,128)S(1)}, f32[35,35]{0,1:T(8,128)S(1)}, f32[35,35]{0,1:T(8,128)S(1)}, /*index=5*/f32[35,35]{...) while((s32[]{:T(128)}, f32[1]{0:T(128)}, ...), condition=%wide.region_15.22_spmd.clone, body=%wide.region_14.21_spmd.clone.sunk | while | flops 28780052 | bytes 1147034 | solution.py:110
  812.7 6.4 cholesky.800
  834.8 6.4 cholesky.800
  856.9 6.4 cholesky.800
  878.9 6.4 cholesky.800
  901.0 6.4 cholesky.800
  923.1 6.4 cholesky.800
  945.1 6.4 cholesky.800
  967.2 6.4 cholesky.800
  1055.4 6.4 cholesky.800
  1196.5 10.8 collective-permute-start.8
  1211.8 16.0 all-gather.6
  1227.8 34.1 %gather_fusion.1 = f32[4480]{0:T(1024)S(1)} fusion(f32[35,2048]{1,0:T(8,128)S(1)} %bitcast.963, s32[4480]{0:T(1024)S(1)} %fusion.351), kind=kCustom, calls=%fused_computation.1.clone | custom fusion | bytes 71680 | tf_op jit(solution)/shard_map/jit(take_along_axis)/gather | solution.py:195
  1266.7 7.7 while.246
  1274.8 21.2 %all-gather.14 = f32[16,35,128]{2,1,0:T(8,128)S(1)} all-gather(f32[1,35,128]{2,1,0:T(8,128)S(1)} %get-tuple-element.2748), channel_id=9, replica_groups=mesh['axial'=16,'pitch'=16] {'axial'}, dimensions={0}, use_global_device_ids=true | all-gather | bytes 304640 | tf_op jit(solution)/shard_map/all_gather | solution.py:225
  1296.0 15.9 all-gather.15
  1311.9 359.7 %while.250 = (s32[]{:T(128)}, f32[1]{0:T(128)}, f32[35,35]{0,1:T(8,128)S(1)}, f32[35,35]{0,1:T(8,128)S(1)}, f32[35,35]{0,1:T(8,128)S(1)}, /*index=5*/f32[35,128]...) while((s32[]{:T(128)}, f32[1]{0:T(128)}, ...), condition=%wide.region_25.32_spmd.clone, body=%wide.region_24.31_spmd.clone.sunk | while | flops 28767804 | bytes 1393563 | solution.py:124
  1316.6 6.4 cholesky.836
  1339.0 6.4 cholesky.836
  1361.5 6.4 cholesky.836
  1383.9 6.4 cholesky.836
  1406.4 6.4 cholesky.836
  1428.9 6.4 cholesky.836
  1451.3 6.4 cholesky.836
  1473.8 6.4 cholesky.836
  1496.3 6.4 cholesky.836
  1518.7 6.4 cholesky.836
  1541.2 6.4 cholesky.836
  1563.7 6.4 cholesky.836
  1586.1 6.4 cholesky.836
  1608.6 6.4 cholesky.836
  1631.0 6.4 cholesky.836
  1653.5 6.4 cholesky.836
  1688.3 325.6 %while.249 = (s32[]{:T(128)}, f32[1]{0:T(128)}, f32[35,35]{0,1:T(8,128)S(1)}, f32[35,35]{0,1:T(8,128)S(1)}, f32[35,35]{0,1:T(8,128)S(1)}, /*index=5*/f32[35,35]{...) while((s32[]{:T(128)}, f32[1]{0:T(128)}, ...), condition=%wide.region_23.30_spmd.clone, body=%wide.region_22.29_spmd.clone.sunk | while | flops 28780052 | bytes 1149594 | solution.py:110
  (2830 shorter events, 1286.7 us)
Async XLA Ops:
  1.0 68.2 %collective-permute-start = (f32[35,35]{1,0:T(8,128)S(1)}, f32[35,35]{1,0:T(8,128)S(1)}, u32[]{:S(2)}, u32[]{:S(2)}) collective-permute-start(f32[35,35]{1,0:T(8,128)S(1)} %get-tuple-element.2740), channel_id=1, source_target_pairs={{0,16},{16,32},{32,48},{48,64},{64,80},{80,96},{96,112},{112,128},... | collective-permute-start | bytes 14708 | tf_op jit(solution)/shard_map/ppermute | solution.py:16
  3.0 214.9 %collective-permute-start.1 = (f32[1,35,128]{2,1,0:T(8,128)}, f32[1,35,128]{2,1,0:T(8,128)S(1)}, u32[]{:S(2)}, u32[]{:S(2)}) collective-permute-start(f32[1,35,128]{2,1,0:T(8,128)} %get-tuple-element.2744), channel_id=1, source_target_pairs={{0,16},{16,32},{32,48},{48,64},{64,80},{80,96},{96,112},{112,128},... | collective-permute-start | bytes 53768 | tf_op jit(solution)/shard_map/ppermute | solution.py:26
  5.1 8.5 copy-start.55
  5.1 296.7 %collective-permute-start.4 = (f32[8,35,1]{2,1,0:T(8,128)}, f32[8,35,1]{2,1,0:T(8,128)}, u32[]{:S(2)}, u32[]{:S(2)}) collective-permute-start(f32[8,35,1]{2,1,0:T(8,128)} %get-tuple-element.2746), channel_id=1, source_target_pairs={{1,0},{2,1},{3,2},{4,3},{5,4},{6,5},{7,6},{8,7},{9,8},{10,9},{11,1... | collective-permute-start | bytes 3368 | tf_op jit(solution)/shard_map/ppermute | solution.py:27
  5.8 296.0 %collective-permute-start.3 = (f32[8,35,1]{2,1,0:T(8,128)}, f32[8,35,1]{2,1,0:T(8,128)}, u32[]{:S(2)}, u32[]{:S(2)}) collective-permute-start(f32[8,35,1]{2,1,0:T(8,128)} %get-tuple-element.2745), channel_id=1, source_target_pairs={{0,1},{1,2},{2,3},{3,4},{4,5},{5,6},{6,7},{7,8},{8,9},{9,10},{10,1... | collective-permute-start | bytes 3368 | tf_op jit(solution)/shard_map/ppermute | solution.py:26
  7.3 294.5 %collective-permute-start.2 = (f32[1,35,128]{2,1,0:T(8,128)}, f32[1,35,128]{2,1,0:T(8,128)}, u32[]{:S(2)}, u32[]{:S(2)}) collective-permute-start(f32[1,35,128]{2,1,0:T(8,128)} %get-tuple-element.2743), channel_id=1, source_target_pairs={{16,0},{32,16},{48,32},{64,48},{80,64},{96,80},{112,96},{128,112},... | collective-permute-start | bytes 53768 | tf_op jit(solution)/shard_map/ppermute | solution.py:27
  14.9 48.8 %copy-start.51 = (s32[128]{0:T(128)}, s32[128]{0:T(128)S(1)}, u32[]{:S(2)}) copy-start(s32[128]{0:T(128)S(1)} %dynamic_slice.307) | copy-start | bytes 1540
  63.7 5.1 copy-start.56
  164.0 148.9 %copy-start.5 = (f32[70,70]{1,0:T(8,128)}, f32[70,70]{1,0:T(8,128)S(1)}, u32[]{:S(2)}) copy-start(f32[70,70]{1,0:T(8,128)S(1)} %fusion.296) | copy-start | bytes 58804
  266.0 34.1 %copy-start.52 = (s32[128]{0:T(128)S(1)}, s32[128]{0:T(128)}, u32[]{:S(2)}) copy-start(s32[128]{0:T(128)} %copy-done.51) | copy-start | bytes 1540
  305.0 7.8 copy-start.43
  312.8 39.5 %copy-start.21 = (f32[7,35,128]{2,1,0:T(8,128)}, f32[7,35,128]{2,1,0:T(8,128)S(1)}, u32[]{:S(2)}) copy-start(f32[7,35,128]{2,1,0:T(8,128)S(1)} %get-tuple-element.1590) | copy-start | bytes 376324
  313.7 38.6 %copy-start.31 = (f32[35,35]{0,1:T(8,128)S(1)}, f32[35,35]{0,1:T(8,128)}, u32[]{:S(2)}) copy-start(f32[35,35]{0,1:T(8,128)} %custom-call.49) | copy-start | bytes 14704
  352.3 5.0 copy-start.60
  378.2 6.5 copy-start.60
  405.5 6.5 copy-start.60
  432.8 6.5 copy-start.60
  460.1 6.5 copy-start.60
  487.4 6.5 copy-start.60
  514.7 6.5 copy-start.60
  542.0 6.5 copy-start.60
  565.1 4.2 copy-start.61
  569.3 6.5 copy-start.60
  596.6 6.5 copy-start.60
  623.9 6.5 copy-start.60
  651.2 6.5 copy-start.60
  678.5 6.5 copy-start.60
  705.8 6.5 copy-start.60
  733.1 6.5 copy-start.60
  760.4 6.5 copy-start.60
  793.8 13.2 copy-start.17
  793.8 13.2 copy-start.20
  797.8 9.5 copy-start.3
  797.8 9.5 copy-start.8
  797.9 9.5 copy-start.12
  797.9 9.5 copy-start.14
  797.9 9.5 copy-start.30
  797.9 9.5 copy-start.34
  797.9 9.5 copy-start.36
  797.9 9.5 copy-start.57
  1168.6 8.7 copy-start.39
  1176.8 13.9 copy-start.38
  1194.5 17.3 collective-permute-start.5
  1196.5 66.9 %collective-permute-start.8 = (f32[8,35,1]{2,1,0:T(8,128)}, f32[8,35,1]{2,1,0:T(8,128)}, u32[]{:S(2)}, u32[]{:S(2)}) collective-permute-start(f32[8,35,1]{2,1,0:T(8,128)} %get-tuple-element.2738), channel_id=1, source_target_pairs={{1,0},{2,1},{3,2},{4,3},{5,4},{6,5},{7,6},{8,7},{9,8},{10,9},{11,1... | collective-permute-start | bytes 3368 | tf_op jit(solution)/shard_map/ppermute | solution.py:27
  1207.3 56.1 %collective-permute-start.7 = (f32[8,35,1]{2,1,0:T(8,128)}, f32[8,35,1]{2,1,0:T(8,128)}, u32[]{:S(2)}, u32[]{:S(2)}) collective-permute-start(f32[8,35,1]{2,1,0:T(8,128)} %get-tuple-element.2737), channel_id=1, source_target_pairs={{0,1},{1,2},{2,3},{3,4},{4,5},{5,6},{6,7},{7,8},{8,9},{9,10},{10,1... | collective-permute-start | bytes 3368 | tf_op jit(solution)/shard_map/ppermute | solution.py:26
  1207.4 56.0 %collective-permute-start.6 = (f32[1,35,128]{2,1,0:T(8,128)S(1)}, f32[1,35,128]{2,1,0:T(8,128)S(1)}, u32[]{:S(2)}, u32[]{:S(2)}) collective-permute-start(f32[1,35,128]{2,1,0:T(8,128)S(1)} %get-tuple-element.2735), channel_id=1, source_target_pairs={{16,0},{32,16},{48,32},{64,48},{80,64},{96,80},{112,96},{128,112},... | collective-permute-start | bytes 53768 | tf_op jit(solution)/shard_map/ppermute | solution.py:27
  1227.8 34.2 %copy-start.53 = (s32[128]{0:T(128)S(1)}, s32[128]{0:T(128)}, u32[]{:S(2)}) copy-start(s32[128]{0:T(128)} %copy-done.51) | copy-start | bytes 1540
  1227.8 34.3 %copy-start.23 = (f32[8,35,128]{2,1,0:T(8,128)S(1)}, f32[8,35,128]{2,1,0:T(8,128)}, u32[]{:S(2)}) copy-start(f32[8,35,128]{2,1,0:T(8,128)} %fusion.397) | copy-start | bytes 430084
  1227.8 34.3 %copy-start.49 = (f32[35,35]{1,0:T(8,128)S(1)}, f32[35,35]{1,0:T(8,128)}, u32[]{:S(2)}) copy-start(f32[35,35]{1,0:T(8,128)} %copy-done.48) | copy-start | bytes 14704
  1266.6 7.8 copy-start.41
  1266.7 7.8 copy-start.6
  1274.7 37.2 %copy-start.4 = (f32[35,35]{0,1:T(8,128)S(1)}, f32[35,35]{0,1:T(8,128)}, u32[]{:S(2)}) copy-start(f32[35,35]{0,1:T(8,128)} %copy.639) | copy-start | bytes 14704
  1274.7 37.2 %copy-start.9 = (f32[35,35]{0,1:T(8,128)S(1)}, f32[35,35]{0,1:T(8,128)}, u32[]{:S(2)}) copy-start(f32[35,35]{0,1:T(8,128)} %custom-call.66) | copy-start | bytes 14704
  1274.7 37.2 %copy-start.10 = (f32[35,35]{0,1:T(8,128)S(1)}, f32[35,35]{0,1:T(8,128)}, u32[]{:S(2)}) copy-start(f32[35,35]{0,1:T(8,128)} %copy.637) | copy-start | bytes 14704
  1274.7 37.2 %copy-start.28 = (f32[35,35]{0,1:T(8,128)S(1)}, f32[35,35]{0,1:T(8,128)}, u32[]{:S(2)}) copy-start(f32[35,35]{0,1:T(8,128)} %custom-call.63) | copy-start | bytes 14704
  1274.7 37.2 %copy-start.29 = (f32[35,128]{1,0:T(8,128)S(1)}, f32[35,128]{1,0:T(8,128)}, u32[]{:S(2)}) copy-start(f32[35,128]{1,0:T(8,128)} %custom-call.64) | copy-start | bytes 53764
  1679.5 8.7 copy-start.2
  1679.6 8.7 copy-start.7
  1679.6 8.7 copy-start.11
  1679.6 8.7 copy-start.27
  1679.6 8.7 copy-start.33
  1679.6 8.7 copy-start.35
  1679.6 8.7 copy-start.58
  2021.8 8.6 copy-start.40
  (112 other events, 339.9 us)
where the time goes:
time: 2080 us; the launch traced here: 2050 us
  other arithmetic  1110 us (53%)
  matrix products  268 us (13%)
  blocking collectives  240 us (12%)
  local copies, waits for them, and re-layouts  222 us (11%)
  loops' own time  174 us (8%)
  starting transfers between devices  26.8 us (1%)
    another operation x192, other arithmetic, join(): factor = jnp.linalg.cholesky(middle)  454 us
    another operation x128, other arithmetic, join(): solved = jax.scipy.linalg.cho_solve((factor, True), outer)  384 us
    dot_general x374, matrix products, product(): return jnp.dot(left, right, precision=HIGHEST)  186 us
    another operation x2, loops' own time, fold_upstream(): lax.scan(step, (identity, identity), (stacked, jnp.arange(count, dtype=jn...  89.6 us
    select_n x256, other arithmetic, choose(): jnp.where(flag, upper, lower)  87.9 us
    another operation x2, loops' own time, fold_downstream(): lax.scan(step, (identity, identity), (stacked, jnp.arange(count, dtype=jn...  82.5 us
    another operation x51, other arithmetic, inverse(): factor = jnp.linalg.cholesky(matrix)  69.4 us
    dynamic_slice x256, local copies, waits for them, and re-layouts, fold_upstream(): lax.scan(step, (identity, identity), (stacked, jnp.arange(count, dtype=jn...  69 us
  transfers between devices with their start and end apart: 9, of which 0 were waited for; matrix products, arithmetic and copies ran while one was open for 9% of the time, Pallas kernels for 0%

commit v1 on v0

v1 whole, which is shorter than its diff:
```python
import functools
import math

import jax
import jax.numpy as jnp
import numpy as np
from jax import lax
from jax.experimental import pallas as pl
from jax.experimental.pallas import tpu as pltpu
from jax.sharding import PartitionSpec as P

INST, VARS, B = 7, 5, 35
CELLS, LINES, CHAIN = 8, 128, 8
NI = 256
NR = 288
NF = 384
F32, BF16, I32 = jnp.float32, jnp.bfloat16, jnp.int32
HIGHEST = lax.Precision.HIGHEST
MESH = pl.DeviceIdType.MESH

C_LOW, C_HIGH, G_LOW, G_HIGH = 0.299, 5.51, 0.00109, 0.00352
LOCAL_STEPS, REDUCED_STEPS = 7, 7


def scalar_bounds(stator):
    ends = []
    for c, g in ((C_LOW, G_LOW), (C_HIGH, G_HIGH)):
        n = CELLS * CHAIN
        t = np.diag(np.full(n, 2 * c + g)) - c * np.eye(n, k=1) - c * np.eye(n, k=-1)
        if not stator:
            t[0, 0] -= c
        keep = np.arange(0, n, CELLS)
        rest = np.setdiff1d(np.arange(n), keep)
        s = t[np.ix_(keep, keep)] - t[np.ix_(keep, rest)] @ np.linalg.solve(
            t[np.ix_(rest, rest)], t[np.ix_(rest, keep)]
        )
        ends.append(np.linalg.eigvalsh(s))
    return float(ends[0][0]), float(ends[1][-1])


def local_bounds():
    bend = 2 * math.cos(math.pi / CELLS)
    return C_LOW * (2 - bend) + G_LOW, C_HIGH * (2 + bend) + G_HIGH


def plan(bounds, steps):
    low, high = bounds
    mid, half = 0.5 * (high + low), 0.5 * (high - low)
    t = first = mid / half
    for _ in range(steps):
        t = 2 * t * t - 1
    return mid, half, first, 1.0 / t


def dot(a, b, precision=None, dims=((1,), (0,))):
    return lax.dot_general(a, b, (dims, ((), ())), precision=precision, preferred_element_type=F32)


def split(x):
    high = x.astype(BF16)
    return high, (x - high.astype(F32)).astype(BF16)


def dot3(a, b):
    (ah, al), (bh, bl) = a, b
    return dot(ah, bh) + (dot(ah, bl) + dot(al, bh))


def iota(shape, axis):
    return lax.broadcasted_iota(I32, shape, axis)


def block_of(index, count):
    return sum(((index >= B * k).astype(I32) for k in range(1, count)), jnp.zeros_like(index))


def ones(mask):
    return jnp.where(mask, 1.0, 0.0).astype(F32)


def chebyshev(n, start, first, lhs, rhs, y_ref, t_ref, steps):
    def step(_, t):
        th, tl = split(t_ref[...])
        yh, yl = split(y_ref[...])
        lhs[0:n, 0:n] = th
        lhs[n : 2 * n, 0:n] = yh
        lhs[2 * n : 3 * n, 0:n] = tl
        lhs[3 * n : 4 * n, 0:n] = yl
        rhs[0:n, 0:n] = th
        rhs[n : 2 * n, 0:n] = tl
        big = dot(lhs[0 : 4 * n, 0:n], rhs[0:n, 0:n])
        small = dot(lhs[0 : 2 * n, 0:n], rhs[n : 2 * n, 0:n])
        square = big[0:n] + (big[2 * n : 3 * n] + small[0:n])
        mixed = big[n : 2 * n] + (big[3 * n : 4 * n] + small[n : 2 * n])
        eye = ones(iota((n, n), 0) == iota((n, n), 1))
        t_ref[...] = 2.0 * square - eye
        y_ref[...] = 2.0 * (t * y_ref[...] + mixed)
        return 2.0 * t * t - 1.0

    lax.fori_loop(0, steps, step, first)


def kernel(
    pitches,
    field_ref, source_ref, couple_ref, shift_ref, gain_ref, map_ref, slide_ref,
    out_ref,
    f_ref, s_ref, r_ref, cl_ref, cr_ref, smat, ymat, tmat, lhs, rhs, xw_h, xw_l, w_h, w_l, u_ref,
    rmat, yred, tred, yt_h, yt_l, qq, pa, pb, hot, xin,
    edge_send, edge_recv, kq, ab, f63, f63_out, f64, f64_out, c63,
    kq_s, kq_r, ab_s, ab_r, ed_s, ed_r, f63_s, f63_r, fw_s, fw_r, f64_s, f64_r, c63_s, c63_r,
):
    p, q = lax.axis_index("axial"), lax.axis_index("pitch")
    l = lax.rem(p, CHAIN)
    base = p - l
    stator = base > 0
    outlet, inlet = p == CHAIN - 1, p == CHAIN
    zs = pitches // 2
    core = lax.rem(q, 2)
    z = q // 2
    left, right = lax.rem(q + pitches - 1, pitches), lax.rem(q + 1, pitches)

    def at(axial, pitch):
        return {"axial": axial, "pitch": pitch}

    def remote(src, dst, send, recv, axial, pitch):
        return pltpu.make_async_remote_copy(
            src_ref=src, dst_ref=dst, send_sem=send, recv_sem=recv,
            device_id=at(axial, pitch), device_id_type=MESH,
        )

    barrier = pltpu.get_barrier_semaphore()

    def greet(axial, pitch):
        pl.semaphore_signal(barrier, inc=1, device_id=at(axial, pitch), device_id_type=MESH)

    for d in range(1, CHAIN):
        greet(base + lax.rem(l + d, CHAIN), q)
    greet(p, left)
    greet(p, right)

    @pl.when(outlet)
    def _():
        greet(p + 1, q)

    @pl.when(inlet)
    def _():
        for d in range(zs):
            greet(p - 1, 2 * lax.rem(z + d, zs) + core)

    row = iota((NF, 1), 0)
    row_block = jnp.where(row < 245, block_of(row, 7), 0)
    in_sep = jnp.logical_and(row >= NI, row < NI + B)
    row_off = jnp.where(in_sep, row - NI, row - B * row_block)
    row_cell = jnp.where(row < 245, row_block + 1, jnp.where(in_sep, 0, -1))
    lane = iota((1, LINES), 1)

    def stack(dst, src):
        dst[240:NF, :] = jnp.zeros((NF - 240, LINES), F32)
        for m in range(7):
            dst[B * m : B * m + B, :] = src[m + 1]
        dst[NI : NI + B, :] = src[0]

    stack(f_ref, field_ref)

    def place_edges(t):
        pick = jnp.logical_or(
            jnp.logical_and(iota((8, LINES), 0) == 0, iota((8, LINES), 1) == 0),
            jnp.logical_and(iota((8, LINES), 0) == 1, iota((8, LINES), 1) == LINES - 1),
        )
        edge_send[t] = dot(ones(pick), f_ref[...], HIGHEST, ((1,), (1,)))

    place_edges(0)

    pl.semaphore_wait(barrier, CHAIN + 1 + jnp.where(outlet, zs, 0) + jnp.where(inlet, 1, 0))

    def edge_copies(t):
        return (
            remote(edge_send.at[t], edge_recv.at[t, 1], ed_s.at[t, 0], ed_r.at[t, 1], p, left),
            remote(edge_send.at[t], edge_recv.at[t, 0], ed_s.at[t, 1], ed_r.at[t, 0], p, right),
        )

    def f63_copies(t):
        src = field_ref.at[CELLS - 1] if t == 0 else f63_out
        return [
            remote(src, f63.at[t, core, z], f63_s.at[t, d], f63_r.at[t, d], p + 1, 2 * lax.rem(z + d, zs) + core)
            for d in range(zs)
        ]

    def f63_arrivals(t):
        src = field_ref.at[CELLS - 1] if t == 0 else f63_out
        return [
            remote(src, f63.at[t, core, lax.rem(z + zs - d, zs)], f63_s.at[t, d], f63_r.at[t, d], p - 1, q)
            for d in range(zs)
        ]

    def forward_copy(t):
        return remote(f63.at[t, core], f63.at[t, core], fw_s.at[t], fw_r.at[t], p, q + 1 - 2 * core)

    def forward_arrival(t):
        return remote(f63.at[t, 1 - core], f63.at[t, 1 - core], fw_s.at[t], fw_r.at[t], p, q + 1 - 2 * core)

    def f64_copy(t):
        src = field_ref.at[0] if t == 0 else f64_out
        return remote(src, f64.at[t], f64_s.at[t], f64_r.at[t], p - 1, q)

    def f64_arrival(t):
        src = field_ref.at[0] if t == 0 else f64_out
        return remote(src, f64.at[t], f64_s.at[t], f64_r.at[t], p + 1, q)

    def c63_copy(to):
        return remote(couple_ref.at[CELLS - 1], c63, c63_s, c63_r, to, q)

    def kq_copies():
        return [
            remote(kq.at[l], kq.at[l], kq_s.at[d], kq_r.at[d], base + lax.rem(l + d, CHAIN), q)
            for d in range(1, CHAIN)
        ]

    def kq_arrivals():
        peers = [lax.rem(l + CHAIN - d, CHAIN) for d in range(1, CHAIN)]
        return [remote(kq.at[s], kq.at[s], kq_s.at[d + 1], kq_r.at[d + 1], base + s, q) for d, s in enumerate(peers)]

    def ab_copies(t):
        return [
            remote(ab.at[t, l], ab.at[t, l], ab_s.at[t, d], ab_r.at[t, d], base + lax.rem(l + d, CHAIN), q)
            for d in range(1, CHAIN)
        ]

    def ab_arrivals(t):
        peers = [lax.rem(l + CHAIN - d, CHAIN) for d in range(1, CHAIN)]
        return [
            remote(ab.at[t, s], ab.at[t, s], ab_s.at[t, d + 1], ab_r.at[t, d + 1], base + s, q)
            for d, s in enumerate(peers)
        ]

    def send_fields(t):
        @pl.when(outlet)
        def _():
            for copy in f63_copies(t):
                copy.start()

        @pl.when(inlet)
        def _():
            f64_copy(t).start()

        for copy in edge_copies(t):
            copy.start()

    def forward(t):
        @pl.when(inlet)
        def _():
            for copy in f63_arrivals(t):
                copy.wait_recv()
            forward_copy(t).start()

    send_fields(0)

    @pl.when(outlet)
    def _():
        c63_copy(p + 1).start()

    stack(s_ref, source_ref)
    pick_cell = ones(row_cell == iota((NF, CELLS), 1))
    own = row_off == iota((NF, B), 1)
    gain_col = jnp.sum(jnp.where(own, dot(pick_cell, gain_ref[...], HIGHEST), 0.0), 1, keepdims=True)
    shift_col = jnp.sum(jnp.where(own, dot(pick_cell, shift_ref[...], HIGHEST), 0.0), 1, keepdims=True)
    g_col = shift_col + 2.0 * gain_col

    @pl.when(inlet)
    def _():
        lines = map_ref[pl.ds(q, 1), :]
        xin[...] = jnp.zeros_like(xin)
        for a in range(INST):
            found = lax.rem(lines + slide_ref[a], pitches * LINES)
            hot[a] = ones(iota((LINES, LINES), 0) == lax.rem(found, LINES)).astype(BF16)

    cl_ref[240:NI, :] = jnp.zeros((NI - 240, B), F32)
    cr_ref[240:NI, :] = jnp.zeros((NI - 240, B), F32)
    for m in range(7):
        cl_ref[B * m : B * m + B, :] = couple_ref[m]
        cr_ref[B * m : B * m + B, :] = couple_ref[m + 1]
    col = iota((1, NI), 1)
    col_block = block_of(col, 8)
    tile = ones(iota((B, NI), 0) == col - B * col_block)
    rep_l = dot(cl_ref[...], tile, HIGHEST)
    rep_r = dot(cr_ref[...], tile, HIGHEST)
    in_block = block_of(iota((NI, 1), 0), 8)
    mid, half, first, scale = plan(local_bounds(), LOCAL_STEPS)
    g_in = g_col[0:NI]
    same = iota((NI, NI), 0) == iota((NI, NI), 1)
    s_full = jnp.where(in_block == col_block, rep_l + rep_r, 0.0)
    s_full -= jnp.where(col_block == in_block + 1, rep_r, 0.0)
    s_full -= jnp.where(col_block + 1 == in_block, rep_l, 0.0)
    s_full += jnp.where(same, jnp.where(iota((NI, 1), 0) < 245, g_in, mid), 0.0)
    s_full = jnp.where(jnp.logical_and(in_block == 7, jnp.logical_not(same)), 0.0, s_full)
    s_full = jnp.where(jnp.logical_and(col_block == 7, jnp.logical_not(same)), 0.0, s_full)
    smat[...] = s_full
    tmat[...] = jnp.where(same, mid - s_full, -s_full) * (1.0 / half)
    ymat[...] = jnp.where(same, 1.0 / half, 0.0)
    links = jnp.where(jnp.logical_and(in_block == 0, col_block == 0), rep_l, 0.0)
    links += jnp.where(jnp.logical_and(in_block == 6, col_block == 1), rep_r, 0.0)
    links = links[:, 0:128]
    links += jnp.where(iota((NI, 128), 1) == row_off[0:NI] + 2 * B, g_in, 0.0)
    chebyshev(NI, 0, jnp.asarray(first, F32), lhs, rhs, ymat, tmat, LOCAL_STEPS)
    x0 = ymat[...] * scale
    ymat[...] = x0
    rest = jnp.where(same, 1.0, 0.0) - dot(smat[...], ymat[...], HIGHEST)
    inv = x0 + dot(x0.astype(BF16), rest.astype(BF16))
    ymat[...] = inv
    forward(0)
    w = dot(ymat[...], links, HIGHEST)
    xw_h[0:NI], xw_l[0:NI] = split(inv)
    xw_h[NI:NF], xw_l[NI:NF] = split(w.T)
    w_h[...], w_l[...] = split(w)
    u_ref[...] = dot(links.T, w, HIGHEST)

    fr, to = iota((128, 128), 0), iota((128, 128), 1)
    top = ones(jnp.logical_or(
        jnp.logical_and(to < B, jnp.logical_or(fr == to + B, fr == to + 2 * B)),
        jnp.logical_and(jnp.logical_and(to >= B, to < 2 * B), fr == to),
    ))
    low = ones(jnp.logical_and(
        jnp.logical_and(to >= 2 * B, to < 3 * B), jnp.logical_or(fr == to - 2 * B, fr == to)
    ))
    sep_g = g_col[NI : NI + 40]
    part = dot(u_ref[0:40, :], top, HIGHEST) + dot(u_ref[B : B + 40, :], low, HIGHEST)
    part += jnp.where(iota((40, 128), 0) == iota((40, 128), 1), sep_g, 0.0)
    kq[l] = part

    @pl.when(inlet)
    def _():
        c63_copy(p - 1).wait_recv()
        kq[l, 0:B, 0:B] = kq[l, 0:B, 0:B] + c63[...]

    for copy in kq_copies():
        copy.start()

    def right_side(t):
        for copy in reversed(edge_copies(t)):
            copy.wait_recv()
        spot = jnp.logical_or(
            jnp.logical_and(iota((16, LINES), 0) == 1, iota((16, LINES), 1) == 0),
            jnp.logical_and(iota((16, LINES), 0) == 8, iota((16, LINES), 1) == LINES - 1),
        )
        sides = dot(edge_recv[t].reshape(16, NF), ones(spot), HIGHEST, ((0,), (0,)))
        f = f_ref[...]
        near = jnp.where(lane == 0, 0.0, pltpu.roll(f, 1, 1)) + jnp.where(
            lane == LINES - 1, 0.0, pltpu.roll(f, LINES - 1, 1)
        )
        r_ref[...] = s_ref[...] + gain_col * (near + sides)

        @pl.when(outlet)
        def _():
            f64_arrival(t).wait_recv()
            r_ref[210:245, :] = r_ref[210:245, :] + dot(couple_ref[CELLS - 1], f64[t], HIGHEST)

    def reach(t):
        forward_arrival(t).wait_recv()
        lines = map_ref[pl.ds(q, 1), :]
        pieces = []
        for a in range(INST):
            for c in range(2):
                xin[a, :, c, 0:VARS, :] = f63[t, c, :, VARS * a : VARS * a + VARS, :]
            high, low_part = split(xin[a].reshape(pitches * 8, LINES))
            found = lax.rem(lines + slide_ref[a], pitches * LINES) // LINES
            got = (dot(high, hot[a]) + dot(low_part, hot[a])).reshape(pitches, 8, LINES)
            which = iota((pitches, 1, LINES), 0) == found.reshape(1, 1, LINES)
            pieces.append(jnp.sum(jnp.where(which, got, 0.0), 0)[0:VARS])
        for a in range(INST):
            u_ref[VARS * a : VARS * a + VARS, :] = pieces[a]
        return dot(c63[...], u_ref[0:B, :], HIGHEST)

    def send_sides(t):
        rh, rl = split(r_ref[0:NI, :])
        both = dot3((xw_h[...], xw_l[...]), (rh, rl))
        r_ref[0:NI, :] = both[0:NI]
        ends = both[NI:NF] + r_ref[NI:NF, :]
        ab[t, l] = ends[0:72]

        @pl.when(inlet)
        def _():
            ab[t, l, 0:B, :] = ab[t, l, 0:B, :] + reach(t)

        for copy in ab_copies(t):
            copy.start()

    def finish(t):
        for copy in ab_arrivals(t):
            copy.wait_recv()
        pb[0:B, :] = jnp.zeros((B, LINES), F32)
        pa[B * CHAIN : NR, :] = jnp.zeros((NR - B * CHAIN, LINES), F32)
        for s in range(CHAIN):
            pa[B * s : B * s + B, :] = ab[t, s, 0:B, :]
            pb[B * s + B : B * s + 2 * B, :] = ab[t, s, B : 2 * B, :]
        ends = dot3((yt_h[...], yt_l[...]), split(pa[...] + pb[0:NR, :]))
        f_ref[0:NI, :] = r_ref[0:NI, :] + dot3((w_h[...], w_l[...]), split(ends))
        f_ref[NI:NF, :] = ends

    right_side(0)
    send_sides(0)

    for copy in kq_arrivals():
        copy.wait_recv()
    qq[0:B, 128:256] = jnp.zeros((B, 128), F32)
    qq[B * CHAIN : NR, :] = jnp.zeros((NR - B * CHAIN, 256), F32)
    for s in range(CHAIN):
        qq[B * s : B * s + B, 0:128] = kq[s, 0:B, :]
        if s + 1 < CHAIN:
            qq[B * s + B : B * s + 2 * B, 128:256] = kq[s, 0:B, :]
    rcol, rrow = iota((1, NR), 1), iota((NR, 1), 0)
    rcol_block, rrow_block = block_of(rcol, 9), block_of(rrow, 9)
    rcol_off, rrow_off = rcol - B * rcol_block, rrow - B * rrow_block
    source_row = iota((256, NR), 0)
    diag_tile = ones(jnp.logical_or(source_row == rcol_off, source_row == rcol_off + 128 + 2 * B))
    link_tile = ones(iota((128, NR), 0) == rcol_off + B)
    link_turn = ones(iota((NR, 128), 1) == rrow_off + B)
    diag = dot(qq[...], diag_tile, HIGHEST)
    above = dot(qq[:, 0:128], link_tile, HIGHEST)
    below = dot(link_turn, qq[:, 0:128], HIGHEST, ((1,), (1,)))
    rotor_plan, stator_plan = plan(scalar_bounds(False), REDUCED_STEPS), plan(scalar_bounds(True), REDUCED_STEPS)
    mid, half_inv, first, scale = (
        jnp.where(stator, jnp.asarray(b, F32), jnp.asarray(a, F32))
        for a, b in zip(
            (rotor_plan[0], 1.0 / rotor_plan[1], rotor_plan[2], rotor_plan[3]),
            (stator_plan[0], 1.0 / stator_plan[1], stator_plan[2], stator_plan[3]),
        )
    )
    same = iota((NR, NR), 0) == iota((NR, NR), 1)
    live = jnp.logical_and(rrow_block < CHAIN, rcol_block < CHAIN)
    red = jnp.where(rcol_block == rrow_block, diag, 0.0)
    red -= jnp.where(rcol_block == rrow_block + 1, above, 0.0)
    red -= jnp.where(rcol_block + 1 == rrow_block, below, 0.0)
    red = jnp.where(live, red, jnp.where(same, mid, 0.0))
    rmat[...] = red
    tred[...] = jnp.where(same, mid - red, -red) * half_inv
    yred[...] = jnp.where(same, half_inv, 0.0)
    chebyshev(NR, 0, first, lhs, rhs, yred, tred, REDUCED_STEPS)
    xr = yred[...] * scale
    want = jnp.logical_and(
        jnp.logical_and(iota((128, NR), 1) == iota((128, NR), 0) + B * l, iota((128, NR), 0) < 2 * B),
        iota((128, NR), 1) < B * CHAIN,
    )
    wanted = ones(want)
    xh, xl = split(xr)
    wanted_b = wanted.astype(BF16)
    y0 = dot(wanted_b, xh) + dot(wanted_b, xl)
    rest = wanted - dot(y0, rmat[...], HIGHEST)
    yt_h[...], yt_l[...] = split(y0 + dot(rest.astype(BF16), xh))

    finish(0)

    f63_out[...] = f_ref[210:245, :]
    f64_out[...] = f_ref[NI : NI + B, :]
    place_edges(1)
    send_fields(1)
    right_side(1)
    forward(1)
    send_sides(1)
    finish(1)
    out_ref[0] = f_ref[NI : NI + B, :]
    for m in range(7):
        out_ref[m + 1] = f_ref[B * m : B * m + B, :]

    for t in range(2):
        for copy in edge_copies(t) + tuple(ab_copies(t)):
            copy.wait_send()
    for copy in kq_copies():
        copy.wait_send()

    @pl.when(outlet)
    def _():
        for t in range(2):
            for copy in f63_copies(t):
                copy.wait_send()
        c63_copy(p + 1).wait_send()

    @pl.when(inlet)
    def _():
        for t in range(2):
            forward_copy(t).wait_send()
            f64_copy(t).wait_send()


def body(pitches, field, source, couple, shift, gain, row_map, slide):
    zs = pitches // 2
    vmem = pl.BlockSpec(memory_space=pltpu.VMEM)
    dma = pltpu.SemaphoreType.DMA
    V = pltpu.VMEM
    return pl.pallas_call(
        functools.partial(kernel, pitches),
        out_shape=jax.ShapeDtypeStruct(field.shape, F32),
        in_specs=[vmem] * 6 + [pl.BlockSpec(memory_space=pltpu.SMEM)],
        out_specs=vmem,
        scratch_shapes=[
            V((NF, LINES), F32), V((NF, LINES), F32), V((NF, LINES), F32),
            V((NI, B), F32), V((NI, B), F32),
            V((NI, NI), F32), V((NI, NI), F32), V((NI, NI), F32),
            V((4 * NR, NR), BF16), V((2 * NR, NR), BF16),
            V((NF, NI), BF16), V((NF, NI), BF16),
            V((NI, 128), BF16), V((NI, 128), BF16),
            V((128, 128), F32),
            V((NR, NR), F32), V((NR, NR), F32), V((NR, NR), F32),
            V((128, NR), BF16), V((128, NR), BF16),
            V((NR, 256), F32),
            V((NR, LINES), F32), V((B * (CHAIN + 1) + 5, LINES), F32),
            V((INST, LINES, LINES), BF16),
            V((INST, zs, 2, 8, LINES), F32),
            V((2, 8, NF), F32), V((2, 2, 8, NF), F32),
            V((CHAIN, 40, 128), F32),
            V((2, CHAIN, 72, LINES), F32),
            V((2, 2, zs, B, LINES), F32), V((B, LINES), F32),
            V((2, B, LINES), F32), V((B, LINES), F32),
            V((B, B), F32),
            dma((CHAIN,)), dma((CHAIN,)), dma((2, CHAIN)), dma((2, CHAIN)),
            dma((2, 2)), dma((2, 2)), dma((2, zs)), dma((2, zs)),
            dma((2,)), dma((2,)), dma((2,)), dma((2,)), dma, dma,
        ],
        compiler_params=pltpu.CompilerParams(
            collective_id=0, has_side_effects=True, vmem_limit_bytes=48 * 2**20
        ),
        name="sweeps",
    )(field, source, couple, shift, gain, row_map.reshape(pitches, LINES), slide)


def solution(mesh):
    return jax.shard_map(
        functools.partial(body, mesh.shape["pitch"]),
        mesh=mesh,
        in_specs=(
            P("axial", None, "pitch"),
            P("axial", None, "pitch"),
            P("axial", None, None),
            P("axial", None),
            P("axial", None),
            P(),
            P(),
        ),
        out_specs=P("axial", None, "pitch"),
        check_vma=False,
    )
```

time: 2080 us -> 48.1 us (0.02); the launches traced: 2050 us -> 47.9 us
  other arithmetic: 1110 us -> 0 us
  matrix products: 268 us -> 0 us
  blocking collectives: 240 us -> 0 us
  local copies, waits for them, and re-layouts: 222 us -> 3.27 us
  loops' own time: 174 us -> 0 us
  Pallas kernels: 0 us -> 44.6 us
  starting transfers between devices: 26.8 us -> 0 us
    another operation x417 -> x0, other arithmetic: 993 us -> none  [the longest x192 454 us: join(): factor = jnp.linalg.cholesky(middle)]
    all_gather x10 -> x0, blocking collectives: 212 us -> none  [the longest x2 64.1 us: body(): gathered = lax.all_gather(padded[0], 'pitch', axis=1, tiled=True)]
    dot_general x382 -> x0, matrix products: 195 us -> none  [the longest x374 186 us: product(): return jnp.dot(left, right, precision=HIGHEST)]
    another operation x11 -> x0, loops' own time: 174 us -> none  [the longest x2 89.6 us: fold_upstream(): lax.scan(step, (identity, identity), (stacked, jnp.arange(count, dtype=jn...]
    select_n x256 -> x0, other arithmetic: 87.9 us -> none  [choose(): jnp.where(flag, upper, lower)]
    another operation x294 -> x0, matrix products: 73.1 us -> none  [the longest x128 31.3 us: join(): solved = jax.scipy.linalg.cho_solve((factor, True), outer)]
    dynamic_slice x257 -> x0, local copies, waits for them, and re-layouts: 69.8 us -> none  [the longest x256 69 us: fold_upstream(): lax.scan(step, (identity, identity), (stacked, jnp.arange(count, dtype=jn...]
    gather x2 -> x0, local copies, waits for them, and re-layouts: 68.3 us -> none  [body(): mapped = jnp.take_along_axis(gathered, lookup, axis=1)]
  transfers between devices with their start and end apart: 9 -> 0, of which waited for: 0 -> 0; matrix products, arithmetic and copies ran while one was open for 9% -> 0% of each run, Pallas kernels for 0% -> 0%
where the time goes in v1:
time: 48.1 us; the launch traced here: 47.9 us
  Pallas kernels  44.6 us (93%)
  local copies, waits for them, and re-layouts  3.27 us (7%)
    pallas_call x1, Pallas kernels, body(): pl.pallas_call(functools.partial(kernel, pitches), out_shape=jax.ShapeDty...  44.6 us
    unnamed x15, local copies, waits for them, and re-layouts  2.58 us

profile of v1, /device:TPU:31, one launch (start us, length us, event | category | flops | bytes accessed | tf_op | source)
XLA Modules:
  0.0 47.9 jit_solution(4888594977744743366)
XLA Ops:
  0.0 0.0 copy-start.4
  0.0 1.0 %copy.8.field_ref = f32[8,35,128]{2,1,0:T(8,128)S(1)} copy(f32[8,35,128]{2,0,1:T(8,128)} %param.7) | data formatting | bytes 286720 | tf_op args[0]
  1.0 0.0 copy-done.4
  1.0 0.0 copy-start.5
  1.0 0.9 %copy-done.5 = f32[8,35,35]{2,0,1:T(8,128)S(1)} copy-done((f32[8,35,35]{2,0,1:T(8,128)S(1)}, f32[8,35,35]{2,0,1:T(8,128)}, u32[]{:S(2)}) %copy-start.5) | copy-done | bytes 39224
  1.9 0.0 copy-start
  1.9 0.0 copy-start.1
  1.9 0.0 copy-start.2
  1.9 0.0 copy-start.3
  2.0 0.6 %copy-done = s32[2048]{0:T(1024)S(1)} copy-done((s32[2048]{0:T(1024)S(1)}, s32[2048]{0:T(1024)}, u32[]{:S(2)}) %copy-start) | copy-done | bytes 8216
  2.6 0.0 copy-done.1
  2.6 0.0 copy-done.2
  2.6 0.0 copy-done.3
  2.6 44.6 %sweeps.1 = f32[8,35,128]{2,1,0:T(8,128)S(1)} custom-call(f32[8,35,128]{2,1,0:T(8,128)S(1)} %copy.8.field_ref, f32[8,35,128]{2,1,0:T(8,128)S(1)} %copy.9.source_ref, f32[8,35,35]{2,1,0:T(8,128)S(1)} %copy.10.couple_ref, f32[8,35]{1,0:T(8,128)S(1)} %copy-done.1, f32[8,35]{1,0:T(8,128)S(1)} %copy-done.2, s32[16,128]{1,0:T(8,128)S(1)} %bitcast.1, s32[7]{0:T(128)S(1)} %copy-done.3), custom_call_target="tpu_custom_call" | custom-call | tf_op jit(solution)/shard_map/sweeps/pallas_call | solution.py:489
  47.2 0.7 %copy.11 = f32[8,35,128]{2,0,1:T(8,128)} copy(f32[8,35,128]{2,1,0:T(8,128)S(1)} %sweeps.1) | data formatting | bytes 286720 | tf_op jit(solution)/shard_map/sweeps/pallas_call | solution.py:489
  (2 shorter events, 0.1 us)
Async XLA Ops:
  0.0 1.0 %copy-start.4 = (f32[8,35,128]{2,0,1:T(8,128)S(1)}, f32[8,35,128]{2,0,1:T(8,128)}, u32[]{:S(2)}) copy-start(f32[8,35,128]{2,0,1:T(8,128)} %param.8) | copy-start | bytes 430084
  1.0 0.9 %copy-start.5 = (f32[8,35,35]{2,0,1:T(8,128)S(1)}, f32[8,35,35]{2,0,1:T(8,128)}, u32[]{:S(2)}) copy-start(f32[8,35,35]{2,0,1:T(8,128)} %param.9) | copy-start | bytes 117604
  1.9 0.7 %copy-start = (s32[2048]{0:T(1024)S(1)}, s32[2048]{0:T(1024)}, u32[]{:S(2)}) copy-start(s32[2048]{0:T(1024)} %param.12) | copy-start | bytes 24580
  1.9 0.7 %copy-start.1 = (f32[8,35]{1,0:T(8,128)S(1)}, f32[8,35]{1,0:T(8,128)}, u32[]{:S(2)}) copy-start(f32[8,35]{1,0:T(8,128)} %shift_ref.1) | copy-start | bytes 3364
  1.9 0.7 %copy-start.2 = (f32[8,35]{1,0:T(8,128)S(1)}, f32[8,35]{1,0:T(8,128)}, u32[]{:S(2)}) copy-start(f32[8,35]{1,0:T(8,128)} %gain_ref.1) | copy-start | bytes 3364
  1.9 0.7 %copy-start.3 = (s32[7]{0:T(128)S(1)}, s32[7]{0:T(128)}, u32[]{:S(2)}) copy-start(s32[7]{0:T(128)} %slide_ref.1) | copy-start | bytes 88

commit v2 on v1

--- a/solution.py
+++ b/solution.py
@@ -19,7 +19,8 @@
 MESH = pl.DeviceIdType.MESH
 
 C_LOW, C_HIGH, G_LOW, G_HIGH = 0.299, 5.51, 0.00109, 0.00352
-LOCAL_STEPS, REDUCED_STEPS = 7, 7
+LOCAL_STEPS, REDUCED_STEPS = 7, 6
+FIRST_SCALE = 0.5
 
 
 def scalar_bounds(stator):
@@ -30,11 +31,12 @@
         if not stator:
             t[0, 0] -= c
         keep = np.arange(0, n, CELLS)
+        scale = np.where(np.arange(CHAIN) == 0, FIRST_SCALE if stator else 1.0, 1.0)
         rest = np.setdiff1d(np.arange(n), keep)
         s = t[np.ix_(keep, keep)] - t[np.ix_(keep, rest)] @ np.linalg.solve(
             t[np.ix_(rest, rest)], t[np.ix_(rest, keep)]
         )
-        ends.append(np.linalg.eigvalsh(s))
+        ends.append(np.linalg.eigvalsh(scale[:, None] * s * scale[None, :]))
     return float(ends[0][0]), float(ends[1][-1])
 
 
@@ -78,37 +80,60 @@
     return jnp.where(mask, 1.0, 0.0).astype(F32)
 
 
-def chebyshev(n, start, first, lhs, rhs, y_ref, t_ref, steps):
-    def step(_, t):
+def chebyshev(n, t, half_inv, lhs, rhs, y_ref, t_ref, steps, exact):
+    eye = ones(iota((n, n), 0) == iota((n, n), 1))
+    rows = 4 if exact else 3
+
+    def load(with_y):
         th, tl = split(t_ref[...])
-        yh, yl = split(y_ref[...])
         lhs[0:n, 0:n] = th
-        lhs[n : 2 * n, 0:n] = yh
-        lhs[2 * n : 3 * n, 0:n] = tl
-        lhs[3 * n : 4 * n, 0:n] = yl
+        lhs[n : 2 * n, 0:n] = tl
         rhs[0:n, 0:n] = th
         rhs[n : 2 * n, 0:n] = tl
-        big = dot(lhs[0 : 4 * n, 0:n], rhs[0:n, 0:n])
-        small = dot(lhs[0 : 2 * n, 0:n], rhs[n : 2 * n, 0:n])
-        square = big[0:n] + (big[2 * n : 3 * n] + small[0:n])
-        mixed = big[n : 2 * n] + (big[3 * n : 4 * n] + small[n : 2 * n])
-        eye = ones(iota((n, n), 0) == iota((n, n), 1))
+        if with_y and exact:
+            lhs[2 * n : 3 * n, 0:n], lhs[3 * n : 4 * n, 0:n] = split(y_ref[...])
+        elif with_y:
+            lhs[2 * n : 3 * n, 0:n] = y_ref[...].astype(BF16)
+
+    load(False)
+    big = dot(lhs[0 : 2 * n, 0:n], rhs[0:n, 0:n])
+    square = big[0:n] + (big[n : 2 * n] + dot(lhs[0:n, 0:n], rhs[n : 2 * n, 0:n]))
+    y_ref[...] = (2.0 * half_inv) * (t * eye + t_ref[...])
+    t_ref[...] = 2.0 * square - eye
+    t = 2.0 * t * t - 1.0
+
+    def step(_, t):
+        load(True)
+        big = dot(lhs[0 : rows * n, 0:n], rhs[0:n, 0:n])
+        square = big[0:n] + (big[n : 2 * n] + dot(lhs[0:n, 0:n], rhs[n : 2 * n, 0:n]))
+        mixed = big[2 * n : 3 * n]
+        if exact:
+            mixed += big[3 * n : 4 * n] + dot(lhs[2 * n : 3 * n, 0:n], rhs[n : 2 * n, 0:n])
         t_ref[...] = 2.0 * square - eye
         y_ref[...] = 2.0 * (t * y_ref[...] + mixed)
         return 2.0 * t * t - 1.0
 
-    lax.fori_loop(0, steps, step, first)
+    t = lax.fori_loop(0, steps - 2, step, t)
+    load(True)
+    big = dot(lhs[2 * n : rows * n, 0:n], rhs[0:n, 0:n])
+    mixed = big[0:n]
+    if exact:
+        mixed += big[n : 2 * n] + dot(lhs[2 * n : 3 * n, 0:n], rhs[n : 2 * n, 0:n])
+    y_ref[...] = 2.0 * (t * y_ref[...] + mixed)
 
 
 def kernel(
     pitches,
-    field_ref, source_ref, couple_ref, shift_ref, gain_ref, map_ref, slide_ref,
-    out_ref,
-    f_ref, s_ref, r_ref, cl_ref, cr_ref, smat, ymat, tmat, lhs, rhs, xw_h, xw_l, w_h, w_l, u_ref,
-    rmat, yred, tred, yt_h, yt_l, qq, pa, pb, hot, xin,
-    edge_send, edge_recv, kq, ab, f63, f63_out, f64, f64_out, c63,
-    kq_s, kq_r, ab_s, ab_r, ed_s, ed_r, f63_s, f63_r, fw_s, fw_r, f64_s, f64_r, c63_s, c63_r,
+    *refs,
 ):
+    args, (out_ref, *args_v) = refs[:7], refs[7:15]
+    (
+        f_ref, s_ref, r_ref, cl_ref, cr_ref, smat, ymat, tmat, lhs, rhs, xw_h, xw_l, w_h, w_l, u_ref,
+        rmat, yred, tred, yt_h, yt_l, qq, pa, pb, hot, xin,
+        edge_send, edge_recv, kq, ab, f63, f63_out, f64, f64_out, c63, c63_out, late,
+        kq_s, kq_r, ab_s, ab_r, ed_s, ed_r, f63_s, f63_r, fw_s, fw_r, f64_s, f64_r, c63_s, c63_r, late_s, late_r, in_s,
+    ) = refs[15:]
+    field_v, source_v, couple_v, shift_v, gain_v, map_v, slide_v = args_v
     p, q = lax.axis_index("axial"), lax.axis_index("pitch")
     l = lax.rem(p, CHAIN)
     base = p - l
@@ -128,6 +153,10 @@
             device_id=at(axial, pitch), device_id_type=MESH,
         )
 
+    loads = [pltpu.make_async_copy(args[i], args_v[i], in_s.at[i]) for i in range(7)]
+    for load in loads:
+        load.start()
+
     barrier = pltpu.get_barrier_semaphore()
 
     def greet(axial, pitch):
@@ -154,13 +183,21 @@
     row_cell = jnp.where(row < 245, row_block + 1, jnp.where(in_sep, 0, -1))
     lane = iota((1, LINES), 1)
 
+    def cell_of(src, i):
+        return src[pl.ds(i, B, stride=CELLS), :]
+
     def stack(dst, src):
         dst[240:NF, :] = jnp.zeros((NF - 240, LINES), F32)
         for m in range(7):
-            dst[B * m : B * m + B, :] = src[m + 1]
-        dst[NI : NI + B, :] = src[0]
-
-    stack(f_ref, field_ref)
+            dst[B * m : B * m + B, :] = cell_of(src, m + 1)
+        dst[NI : NI + B, :] = cell_of(src, 0)
+
+    loads[0].wait()
+    stack(f_ref, field_v)
+    f63_out[0] = cell_of(field_v, CELLS - 1)
+    f64_out[0] = cell_of(field_v, 0)
+    loads[2].wait()
+    c63_out[...] = cell_of(couple_v, CELLS - 1)
 
     def place_edges(t):
         pick = jnp.logical_or(
@@ -170,7 +207,8 @@
         edge_send[t] = dot(ones(pick), f_ref[...], HIGHEST, ((1,), (1,)))
 
     place_edges(0)
-
+    for i in (1, 3, 4, 5, 6):
+        loads[i].wait()
     pl.semaphore_wait(barrier, CHAIN + 1 + jnp.where(outlet, zs, 0) + jnp.where(inlet, 1, 0))
 
     def edge_copies(t):
@@ -180,14 +218,14 @@
         )
 
     def f63_copies(t):
-        src = field_ref.at[CELLS - 1] if t == 0 else f63_out
+        src = f63_out.at[t]
         return [
             remote(src, f63.at[t, core, z], f63_s.at[t, d], f63_r.at[t, d], p + 1, 2 * lax.rem(z + d, zs) + core)
             for d in range(zs)
         ]
 
     def f63_arrivals(t):
-        src = field_ref.at[CELLS - 1] if t == 0 else f63_out
+        src = f63_out.at[t]
         return [
             remote(src, f63.at[t, core, lax.rem(z + zs - d, zs)], f63_s.at[t, d], f63_r.at[t, d], p - 1, q)
             for d in range(zs)
@@ -200,15 +238,15 @@
         return remote(f63.at[t, 1 - core], f63.at[t, 1 - core], fw_s.at[t], fw_r.at[t], p, q + 1 - 2 * core)
 
     def f64_copy(t):
-        src = field_ref.at[0] if t == 0 else f64_out
+        src = f64_out.at[t]
         return remote(src, f64.at[t], f64_s.at[t], f64_r.at[t], p - 1, q)
 
     def f64_arrival(t):
-        src = field_ref.at[0] if t == 0 else f64_out
+        src = f64_out.at[t]
         return remote(src, f64.at[t], f64_s.at[t], f64_r.at[t], p + 1, q)
 
     def c63_copy(to):
-        return remote(couple_ref.at[CELLS - 1], c63, c63_s, c63_r, to, q)
+        return remote(c63_out, c63, c63_s, c63_r, to, q)
 
     def kq_copies():
         return [
@@ -233,18 +271,29 @@
             for d, s in enumerate(peers)
         ]
 
-    def send_fields(t):
+    def send_inlet(t):
+        @pl.when(inlet)
+        def _():
+            f64_copy(t).start()
+
+    def send_outlet(t):
         @pl.when(outlet)
         def _():
             for copy in f63_copies(t):
                 copy.start()
 
-        @pl.when(inlet)
-        def _():
-            f64_copy(t).start()
-
+    def send_edges(t):
         for copy in edge_copies(t):
             copy.start()
+
+    def late_copies(t):
+        return [
+            remote(late.at[t], late.at[t], late_s.at[t, d], late_r.at[t], base + lax.rem(l + d, CHAIN), q)
+            for d in range(1, CHAIN)
+        ]
+
+    def late_arrival(t):
+        return remote(late.at[t], late.at[t], late_s.at[t, 0], late_r.at[t], base, q)
 
     def forward(t):
         @pl.when(inlet)
@@ -253,32 +302,34 @@
                 copy.wait_recv()
             forward_copy(t).start()
 
-    send_fields(0)
+    send_outlet(0)
+    send_inlet(0)
+    send_edges(0)
 
     @pl.when(outlet)
     def _():
         c63_copy(p + 1).start()
 
-    stack(s_ref, source_ref)
+    stack(s_ref, source_v)
     pick_cell = ones(row_cell == iota((NF, CELLS), 1))
     own = row_off == iota((NF, B), 1)
-    gain_col = jnp.sum(jnp.where(own, dot(pick_cell, gain_ref[...], HIGHEST), 0.0), 1, keepdims=True)
-    shift_col = jnp.sum(jnp.where(own, dot(pick_cell, shift_ref[...], HIGHEST), 0.0), 1, keepdims=True)
+    gain_col = jnp.sum(jnp.where(own, dot(pick_cell, gain_v[...], HIGHEST), 0.0), 1, keepdims=True)
+    shift_col = jnp.sum(jnp.where(own, dot(pick_cell, shift_v[...], HIGHEST), 0.0), 1, keepdims=True)
     g_col = shift_col + 2.0 * gain_col
 
     @pl.when(inlet)
     def _():
-        lines = map_ref[pl.ds(q, 1), :]
+        lines = map_v[pl.ds(q, 1), :]
         xin[...] = jnp.zeros_like(xin)
         for a in range(INST):
-            found = lax.rem(lines + slide_ref[a], pitches * LINES)
+            found = lax.rem(lines + slide_v[:, a : a + 1], pitches * LINES)
             hot[a] = ones(iota((LINES, LINES), 0) == lax.rem(found, LINES)).astype(BF16)
 
     cl_ref[240:NI, :] = jnp.zeros((NI - 240, B), F32)
     cr_ref[240:NI, :] = jnp.zeros((NI - 240, B), F32)
     for m in range(7):
-        cl_ref[B * m : B * m + B, :] = couple_ref[m]
-        cr_ref[B * m : B * m + B, :] = couple_ref[m + 1]
+        cl_ref[B * m : B * m + B, :] = cell_of(couple_v, m)
+        cr_ref[B * m : B * m + B, :] = cell_of(couple_v, m + 1)
     col = iota((1, NI), 1)
     col_block = block_of(col, 8)
     tile = ones(iota((B, NI), 0) == col - B * col_block)
@@ -296,12 +347,11 @@
     s_full = jnp.where(jnp.logical_and(col_block == 7, jnp.logical_not(same)), 0.0, s_full)
     smat[...] = s_full
     tmat[...] = jnp.where(same, mid - s_full, -s_full) * (1.0 / half)
-    ymat[...] = jnp.where(same, 1.0 / half, 0.0)
     links = jnp.where(jnp.logical_and(in_block == 0, col_block == 0), rep_l, 0.0)
     links += jnp.where(jnp.logical_and(in_block == 6, col_block == 1), rep_r, 0.0)
     links = links[:, 0:128]
     links += jnp.where(iota((NI, 128), 1) == row_off[0:NI] + 2 * B, g_in, 0.0)
-    chebyshev(NI, 0, jnp.asarray(first, F32), lhs, rhs, ymat, tmat, LOCAL_STEPS)
+    chebyshev(NI, jnp.asarray(first, F32), 1.0 / half, lhs, rhs, ymat, tmat, LOCAL_STEPS, True)
     x0 = ymat[...] * scale
     ymat[...] = x0
     rest = jnp.where(same, 1.0, 0.0) - dot(smat[...], ymat[...], HIGHEST)
@@ -352,23 +402,29 @@
         @pl.when(outlet)
         def _():
             f64_arrival(t).wait_recv()
-            r_ref[210:245, :] = r_ref[210:245, :] + dot(couple_ref[CELLS - 1], f64[t], HIGHEST)
+            r_ref[210:245, :] = r_ref[210:245, :] + dot(c63_out[...], f64[t], HIGHEST)
 
     def reach(t):
-        forward_arrival(t).wait_recv()
-        lines = map_ref[pl.ds(q, 1), :]
-        pieces = []
+        lines = map_v[pl.ds(q, 1), :]
+        total = [None] * INST
+        for half_at in range(2):
+            c = core if half_at == 0 else 1 - core
+            if half_at == 1:
+                forward_arrival(t).wait_recv()
+            for a in range(INST):
+                xin[a, :, 0:VARS, :] = f63[t, c, :, VARS * a : VARS * a + VARS, :]
+            for a in range(INST):
+                high, low_part = split(xin[a].reshape(zs * 8, LINES))
+                found = lax.rem(lines + slide_v[:, a : a + 1], pitches * LINES) // LINES
+                got = (dot(high, hot[a]) + dot(low_part, hot[a])).reshape(zs, 8, LINES)
+                which = 2 * iota((zs, 1, LINES), 0) + c == found.reshape(1, 1, LINES)
+                piece = jnp.sum(jnp.where(which, got, 0.0), 0)[0:VARS]
+                total[a] = piece if half_at == 0 else total[a] + piece
         for a in range(INST):
-            for c in range(2):
-                xin[a, :, c, 0:VARS, :] = f63[t, c, :, VARS * a : VARS * a + VARS, :]
-            high, low_part = split(xin[a].reshape(pitches * 8, LINES))
-            found = lax.rem(lines + slide_ref[a], pitches * LINES) // LINES
-            got = (dot(high, hot[a]) + dot(low_part, hot[a])).reshape(pitches, 8, LINES)
-            which = iota((pitches, 1, LINES), 0) == found.reshape(1, 1, LINES)
-            pieces.append(jnp.sum(jnp.where(which, got, 0.0), 0)[0:VARS])
-        for a in range(INST):
-            u_ref[VARS * a : VARS * a + VARS, :] = pieces[a]
-        return dot(c63[...], u_ref[0:B, :], HIGHEST)
+            u_ref[VARS * a : VARS * a + VARS, :] = total[a]
+        late[t] = dot(c63[...], u_ref[0:B, :], HIGHEST)
+        for copy in late_copies(t):
+            copy.start()
 
     def send_sides(t):
         rh, rl = split(r_ref[0:NI, :])
@@ -376,11 +432,6 @@
         r_ref[0:NI, :] = both[0:NI]
         ends = both[NI:NF] + r_ref[NI:NF, :]
         ab[t, l] = ends[0:72]
-
-        @pl.when(inlet)
-        def _():
-            ab[t, l, 0:B, :] = ab[t, l, 0:B, :] + reach(t)
-
         for copy in ab_copies(t):
             copy.start()
 
@@ -392,12 +443,28 @@
         for s in range(CHAIN):
             pa[B * s : B * s + B, :] = ab[t, s, 0:B, :]
             pb[B * s + B : B * s + 2 * B, :] = ab[t, s, B : 2 * B, :]
+
+        @pl.when(stator)
+        def _():
+            @pl.when(jnp.logical_not(inlet))
+            def _():
+                late_arrival(t).wait_recv()
+
+            pa[0:B, :] = pa[0:B, :] + late[t]
+
         ends = dot3((yt_h[...], yt_l[...]), split(pa[...] + pb[0:NR, :]))
+        if t == 0:
+            f64_out[1] = ends[0:B]
+            send_inlet(1)
         f_ref[0:NI, :] = r_ref[0:NI, :] + dot3((w_h[...], w_l[...]), split(ends))
         f_ref[NI:NF, :] = ends
 
     right_side(0)
     send_sides(0)
+
+    @pl.when(inlet)
+    def _():
+        reach(0)
 
     for copy in kq_arrivals():
         copy.wait_recv()
@@ -430,36 +497,43 @@
     red = jnp.where(rcol_block == rrow_block, diag, 0.0)
     red -= jnp.where(rcol_block == rrow_block + 1, above, 0.0)
     red -= jnp.where(rcol_block + 1 == rrow_block, below, 0.0)
-    red = jnp.where(live, red, jnp.where(same, mid, 0.0))
+    first_scale = jnp.where(stator, jnp.asarray(FIRST_SCALE, F32), jnp.asarray(1.0, F32))
+    row_scale, col_scale = (jnp.where(i < B, first_scale, 1.0) for i in (rrow, rcol))
+    red = jnp.where(live, red * (row_scale * col_scale), jnp.where(same, mid, 0.0))
     rmat[...] = red
     tred[...] = jnp.where(same, mid - red, -red) * half_inv
-    yred[...] = jnp.where(same, half_inv, 0.0)
-    chebyshev(NR, 0, first, lhs, rhs, yred, tred, REDUCED_STEPS)
+    chebyshev(NR, first, half_inv, lhs, rhs, yred, tred, REDUCED_STEPS, False)
     xr = yred[...] * scale
     want = jnp.logical_and(
         jnp.logical_and(iota((128, NR), 1) == iota((128, NR), 0) + B * l, iota((128, NR), 0) < 2 * B),
         iota((128, NR), 1) < B * CHAIN,
     )
-    wanted = ones(want)
-    xh, xl = split(xr)
-    wanted_b = wanted.astype(BF16)
-    y0 = dot(wanted_b, xh) + dot(wanted_b, xl)
-    rest = wanted - dot(y0, rmat[...], HIGHEST)
-    yt_h[...], yt_l[...] = split(y0 + dot(rest.astype(BF16), xh))
+    wanted = jnp.where(want, col_scale, 0.0)
+    yred[...] = xr
+    y = dot3(split(wanted), split(yred[...]))
+    for _ in range(2):
+        rest = wanted - dot(y, rmat[...], HIGHEST)
+        y += dot(rest.astype(BF16), yred[...].astype(BF16))
+    yt_h[...], yt_l[...] = split(y * col_scale)
 
     finish(0)
 
-    f63_out[...] = f_ref[210:245, :]
-    f64_out[...] = f_ref[NI : NI + B, :]
+    f63_out[1] = f_ref[210:245, :]
+    send_outlet(1)
     place_edges(1)
-    send_fields(1)
+    send_edges(1)
     right_side(1)
+    send_sides(1)
     forward(1)
-    send_sides(1)
+
+    @pl.when(inlet)
+    def _():
+        reach(1)
+
     finish(1)
-    out_ref[0] = f_ref[NI : NI + B, :]
+    out_ref[pl.ds(0, B, stride=CELLS), :] = f_ref[NI : NI + B, :]
     for m in range(7):
-        out_ref[m + 1] = f_ref[B * m : B * m + B, :]
+        out_ref[pl.ds(m + 1, B, stride=CELLS), :] = f_ref[B * m : B * m + B, :]
 
     for t in range(2):
         for copy in edge_copies(t) + tuple(ab_copies(t)):
@@ -479,6 +553,8 @@
         for t in range(2):
             forward_copy(t).wait_send()
             f64_copy(t).wait_send()
+            for copy in late_copies(t):
+                copy.wait_send()
 
 
 def body(pitches, field, source, couple, shift, gain, row_map, slide):
@@ -486,12 +562,14 @@
     vmem = pl.BlockSpec(memory_space=pltpu.VMEM)
     dma = pltpu.SemaphoreType.DMA
     V = pltpu.VMEM
-    return pl.pallas_call(
+    shapes = [(B * CELLS, LINES), (B * CELLS, LINES), (B * CELLS, B), (CELLS, B), (CELLS, B)]
+    shapes = [V(s, F32) for s in shapes] + [V((pitches, LINES), I32), V((1, INST), I32)]
+    out = pl.pallas_call(
         functools.partial(kernel, pitches),
-        out_shape=jax.ShapeDtypeStruct(field.shape, F32),
-        in_specs=[vmem] * 6 + [pl.BlockSpec(memory_space=pltpu.SMEM)],
+        out_shape=jax.ShapeDtypeStruct((B * CELLS, LINES), F32),
+        in_specs=[pl.BlockSpec(memory_space=pltpu.HBM)] * 7,
         out_specs=vmem,
-        scratch_shapes=[
+        scratch_shapes=shapes + [
             V((NF, LINES), F32), V((NF, LINES), F32), V((NF, LINES), F32),
             V((NI, B), F32), V((NI, B), F32),
             V((NI, NI), F32), V((NI, NI), F32), V((NI, NI), F32),
@@ -504,22 +582,29 @@
             V((NR, 256), F32),
             V((NR, LINES), F32), V((B * (CHAIN + 1) + 5, LINES), F32),
             V((INST, LINES, LINES), BF16),
-            V((INST, zs, 2, 8, LINES), F32),
+            V((INST, zs, 8, LINES), F32),
             V((2, 8, NF), F32), V((2, 2, 8, NF), F32),
             V((CHAIN, 40, 128), F32),
             V((2, CHAIN, 72, LINES), F32),
-            V((2, 2, zs, B, LINES), F32), V((B, LINES), F32),
-            V((2, B, LINES), F32), V((B, LINES), F32),
-            V((B, B), F32),
+            V((2, 2, zs, B, LINES), F32), V((2, B, LINES), F32),
+            V((2, B, LINES), F32), V((2, B, LINES), F32),
+            V((B, B), F32), V((B, B), F32), V((2, B, LINES), F32),
             dma((CHAIN,)), dma((CHAIN,)), dma((2, CHAIN)), dma((2, CHAIN)),
             dma((2, 2)), dma((2, 2)), dma((2, zs)), dma((2, zs)),
             dma((2,)), dma((2,)), dma((2,)), dma((2,)), dma, dma,
+            dma((2, CHAIN)), dma((2,)), dma((7,)),
         ],
         compiler_params=pltpu.CompilerParams(
-            collective_id=0, has_side_effects=True, vmem_limit_bytes=48 * 2**20
+            collective_id=0, has_side_effects=True, vmem_limit_bytes=60 * 2**20
         ),
         name="sweeps",
-    )(field, source, couple, shift, gain, row_map.reshape(pitches, LINES), slide)
+    )(
+        field.transpose(1, 0, 2).reshape(B * CELLS, LINES),
+        source.transpose(1, 0, 2).reshape(B * CELLS, LINES),
+        couple.transpose(1, 0, 2).reshape(B * CELLS, B),
+        shift, gain, row_map.reshape(pitches, LINES), slide.reshape(1, INST),
+    )
+    return out.reshape(B, CELLS, LINES).transpose(1, 0, 2)
 
 
 def solution(mesh):

time: 48.1 us -> 43.5 us (0.904)
  the two profiles are of different devices: /device:TPU:31 before, /device:TPU:5 now
where the time goes in v2:
time: 43.5 us; the launch traced here: 43.4 us
  Pallas kernels  41.8 us (96%)
  local copies, waits for them, and re-layouts  1.58 us (4%)
    pallas_call x1, Pallas kernels, body(): pl.pallas_call(functools.partial(kernel, pitches), out_shape=jax.ShapeDty...  41.8 us
    unnamed x1, local copies, waits for them, and re-layouts  1.58 us

profile of v2, /device:TPU:5, one launch (start us, length us, event | category | flops | bytes accessed | tf_op | source)
XLA Modules:
  0.0 43.4 jit_solution(10511348305519940803)
XLA Ops:
  0.0 41.8 %sweeps.1 = f32[280,128]{1,0:T(8,128)} custom-call(f32[280,128]{1,0:T(8,128)} %bitcast.15, f32[280,128]{1,0:T(8,128)} %bitcast.16, f32[280,35]{1,0:T(8,128)} %bitcast.17, f32[8,35]{1,0:T(8,128)} %refs_3_.1, f32[8,35]{1,0:T(8,128)} %refs_4_.1, s32[16,128]{1,0:T(8,128)} %bitcast.18, s32[1,7]{1,0:T(1,128)} %bitcast.19), custom_call_target="tpu_custom_call" | custom-call | tf_op jit(solution)/shard_map/sweeps/pallas_call | solution.py:567
  41.8 1.6 %copy.9 = f32[8,35,128]{2,0,1:T(8,128)} copy(f32[8,35,128]{2,0,1:T(8,128)} %bitcast.14) | data formatting | bytes 286720

commit v3 on v2

--- a/solution.py
+++ b/solution.py
@@ -68,6 +68,16 @@
     return dot(ah, bh) + (dot(ah, bl) + dot(al, bh))
 
 
+def exact(a, pick, dims=((1,), (0,)), swap=False, parts=3):
+    pick, total = pick.astype(BF16), None
+    for _ in range(parts):
+        piece = a.astype(BF16)
+        a = a - piece.astype(F32)
+        term = dot(pick, piece, None, dims) if swap else dot(piece, pick, None, dims)
+        total = term if total is None else total + term
+    return total
+
+
 def iota(shape, axis):
     return lax.broadcasted_iota(I32, shape, axis)
 
@@ -128,10 +138,10 @@
 ):
     args, (out_ref, *args_v) = refs[:7], refs[7:15]
     (
-        f_ref, s_ref, r_ref, cl_ref, cr_ref, smat, ymat, tmat, lhs, rhs, xw_h, xw_l, w_h, w_l, u_ref,
+        f_ref, s_ref, r_ref, g_ref, h_ref, cl_ref, cr_ref, smat, ymat, tmat, lhs, rhs, xw_h, xw_l, w_h, w_l, u_ref,
         rmat, yred, tred, yt_h, yt_l, qq, pa, pb, hot, xin,
-        edge_send, edge_recv, kq, ab, f63, f63_out, f64, f64_out, c63, c63_out, late,
-        kq_s, kq_r, ab_s, ab_r, ed_s, ed_r, f63_s, f63_r, fw_s, fw_r, f64_s, f64_r, c63_s, c63_r, late_s, late_r, in_s,
+        edge_send, edge_recv, kq, ab, corr, pass_out, pass_in, f63, f63_out, f64, f64_out, c63, c63_out, late,
+        kq_s, kq_r, ab_s, ab_r, co_s, co_r, ed_s, ed_r, f63_s, f63_r, fw_s, fw_r, f64_s, f64_r, c63_s, c63_r, late_s, late_r, in_s,
     ) = refs[15:]
     field_v, source_v, couple_v, shift_v, gain_v, map_v, slide_v = args_v
     p, q = lax.axis_index("axial"), lax.axis_index("pitch")
@@ -204,7 +214,7 @@
             jnp.logical_and(iota((8, LINES), 0) == 0, iota((8, LINES), 1) == 0),
             jnp.logical_and(iota((8, LINES), 0) == 1, iota((8, LINES), 1) == LINES - 1),
         )
-        edge_send[t] = dot(ones(pick), f_ref[...], HIGHEST, ((1,), (1,)))
+        edge_send[t] = exact(f_ref[...], ones(pick), ((1,), (1,)), True, 2)
 
     place_edges(0)
     for i in (1, 3, 4, 5, 6):
@@ -220,22 +230,19 @@
     def f63_copies(t):
         src = f63_out.at[t]
         return [
-            remote(src, f63.at[t, core, z], f63_s.at[t, d], f63_r.at[t, d], p + 1, 2 * lax.rem(z + d, zs) + core)
+            remote(src, f63.at[t, z], f63_s.at[t, d], f63_r.at[t, d], p + 1, 2 * lax.rem(z + d, zs) + core)
             for d in range(zs)
         ]
 
     def f63_arrivals(t):
         src = f63_out.at[t]
         return [
-            remote(src, f63.at[t, core, lax.rem(z + zs - d, zs)], f63_s.at[t, d], f63_r.at[t, d], p - 1, q)
+            remote(src, f63.at[t, lax.rem(z + zs - d, zs)], f63_s.at[t, d], f63_r.at[t, d], p - 1, q)
             for d in range(zs)
         ]
 
-    def forward_copy(t):
-        return remote(f63.at[t, core], f63.at[t, core], fw_s.at[t], fw_r.at[t], p, q + 1 - 2 * core)
-
-    def forward_arrival(t):
-        return remote(f63.at[t, 1 - core], f63.at[t, 1 - core], fw_s.at[t], fw_r.at[t], p, q + 1 - 2 * core)
+    def pass_copy(t):
+        return remote(pass_out.at[t], pass_in.at[t], fw_s.at[t], fw_r.at[t], p, q + 1 - 2 * core)
 
     def f64_copy(t):
         src = f64_out.at[t]
@@ -258,18 +265,20 @@
         peers = [lax.rem(l + CHAIN - d, CHAIN) for d in range(1, CHAIN)]
         return [remote(kq.at[s], kq.at[s], kq_s.at[d + 1], kq_r.at[d + 1], base + s, q) for d, s in enumerate(peers)]
 
-    def ab_copies(t):
+    def end_copies(t, ref, send, recv):
         return [
-            remote(ab.at[t, l], ab.at[t, l], ab_s.at[t, d], ab_r.at[t, d], base + lax.rem(l + d, CHAIN), q)
+            remote(ref.at[t, l], ref.at[t, l], send.at[t, d], recv.at[t, d], base + lax.rem(l + d, CHAIN), q)
             for d in range(1, CHAIN)
         ]
 
-    def ab_arrivals(t):
+    def end_arrivals(t, ref, send, recv):
         peers = [lax.rem(l + CHAIN - d, CHAIN) for d in range(1, CHAIN)]
         return [
-            remote(ab.at[t, s], ab.at[t, s], ab_s.at[t, d + 1], ab_r.at[t, d + 1], base + s, q)
+            remote(ref.at[t, s], ref.at[t, s], send.at[t, d + 1], recv.at[t, d + 1], base + s, q)
             for d, s in enumerate(peers)
         ]
+
+    ends_of, corrections = (ab, ab_s, ab_r), (corr, co_s, co_r)
 
     def send_inlet(t):
         @pl.when(inlet)
@@ -293,14 +302,7 @@
         ]
 
     def late_arrival(t):
-        return remote(late.at[t], late.at[t], late_s.at[t, 0], late_r.at[t], base, q)
-
-    def forward(t):
-        @pl.when(inlet)
-        def _():
-            for copy in f63_arrivals(t):
-                copy.wait_recv()
-            forward_copy(t).start()
+        return remote(late.at[t], late.at[t], late_s.at[t, 0], late_r.at[t], jnp.where(stator, CHAIN, CHAIN - 1), q)
 
     send_outlet(0)
     send_inlet(0)
@@ -316,14 +318,23 @@
     gain_col = jnp.sum(jnp.where(own, dot(pick_cell, gain_v[...], HIGHEST), 0.0), 1, keepdims=True)
     shift_col = jnp.sum(jnp.where(own, dot(pick_cell, shift_v[...], HIGHEST), 0.0), 1, keepdims=True)
     g_col = shift_col + 2.0 * gain_col
+    place = iota((1, NF), 1)
+    place_block = jnp.where(place < 245, block_of(place, 7), 0)
+    place_sep = jnp.logical_and(place >= NI, place < NI + B)
+    place_off = jnp.where(place_sep, place - NI, place - B * place_block)
+    place_cell = jnp.where(place < 245, place_block + 1, jnp.where(place_sep, 0, -1))
+    gains = dot(gain_v[...], ones(place_cell == iota((CELLS, NF), 0)), HIGHEST, ((0,), (0,)))
+    gain_row = jnp.sum(jnp.where(place_off == iota((B, NF), 0), gains, 0.0), 0, keepdims=True)
 
     @pl.when(inlet)
     def _():
         lines = map_v[pl.ds(q, 1), :]
         xin[...] = jnp.zeros_like(xin)
-        for a in range(INST):
-            found = lax.rem(lines + slide_v[:, a : a + 1], pitches * LINES)
-            hot[a] = ones(iota((LINES, LINES), 0) == lax.rem(found, LINES)).astype(BF16)
+        other_lines = map_v[pl.ds(q + 1 - 2 * core, 1), :]
+        for whose, wanted_lines in enumerate((lines, other_lines)):
+            for a in range(INST):
+                found = lax.rem(wanted_lines + slide_v[:, a : a + 1], pitches * LINES)
+                hot[whose, a] = ones(iota((LINES, LINES), 0) == lax.rem(found, LINES)).astype(BF16)
 
     cl_ref[240:NI, :] = jnp.zeros((NI - 240, B), F32)
     cr_ref[240:NI, :] = jnp.zeros((NI - 240, B), F32)
@@ -333,8 +344,8 @@
     col = iota((1, NI), 1)
     col_block = block_of(col, 8)
     tile = ones(iota((B, NI), 0) == col - B * col_block)
-    rep_l = dot(cl_ref[...], tile, HIGHEST)
-    rep_r = dot(cr_ref[...], tile, HIGHEST)
+    rep_l = exact(cl_ref[...], tile)
+    rep_r = exact(cr_ref[...], tile)
     in_block = block_of(iota((NI, 1), 0), 8)
     mid, half, first, scale = plan(local_bounds(), LOCAL_STEPS)
     g_in = g_col[0:NI]
@@ -356,13 +367,11 @@
     ymat[...] = x0
     rest = jnp.where(same, 1.0, 0.0) - dot(smat[...], ymat[...], HIGHEST)
     inv = x0 + dot(x0.astype(BF16), rest.astype(BF16))
-    ymat[...] = inv
-    forward(0)
-    w = dot(ymat[...], links, HIGHEST)
     xw_h[0:NI], xw_l[0:NI] = split(inv)
+    w = dot3((xw_h[0:NI], xw_l[0:NI]), split(links))
     xw_h[NI:NF], xw_l[NI:NF] = split(w.T)
     w_h[...], w_l[...] = split(w)
-    u_ref[...] = dot(links.T, w, HIGHEST)
+    u_ref[...] = dot3(split(links.T), (w_h[...], w_l[...]))
 
     fr, to = iota((128, 128), 0), iota((128, 128), 1)
     top = ones(jnp.logical_or(
@@ -373,7 +382,7 @@
         jnp.logical_and(to >= 2 * B, to < 3 * B), jnp.logical_or(fr == to - 2 * B, fr == to)
     ))
     sep_g = g_col[NI : NI + 40]
-    part = dot(u_ref[0:40, :], top, HIGHEST) + dot(u_ref[B : B + 40, :], low, HIGHEST)
+    part = exact(u_ref[0:40, :], top) + exact(u_ref[B : B + 40, :], low)
     part += jnp.where(iota((40, 128), 0) == iota((40, 128), 1), sep_g, 0.0)
     kq[l] = part
 
@@ -385,72 +394,103 @@
     for copy in kq_copies():
         copy.start()
 
-    def right_side(t):
+    def sides(t):
+        f = f_ref[...]
+        near = jnp.where(lane == 0, 0.0, pltpu.roll(f, 1, 1)) + jnp.where(
+            lane == LINES - 1, 0.0, pltpu.roll(f, LINES - 1, 1)
+        )
+        r_ref[...] = s_ref[...] + gain_col * near
+        both = dot3((xw_h[...], xw_l[...]), split(r_ref[0:NI, :]))
+        ab[t, l] = (both[NI:NF] + r_ref[NI:NF, :])[0:72]
+        for copy in end_copies(t, *ends_of):
+            copy.start()
+        r_ref[0:NI, :] = both[0:NI]
+
+    def edges(t):
         for copy in reversed(edge_copies(t)):
             copy.wait_recv()
+        ge = edge_recv[t].reshape(16, NF) * gain_row
+        ge_h, ge_l = split(ge)
+        short = dot3((ge_h[:, 0:NI], ge_l[:, 0:NI]), (w_h[...], w_l[...])) + ge[:, NI:NF]
+        which = iota((8, 128), 0)
+        corr[t, l] = jnp.where(which == 1, short[0:8], 0.0) + jnp.where(which == 0, short[8:16], 0.0)
+        for copy in end_copies(t, *corrections):
+            copy.start()
         spot = jnp.logical_or(
             jnp.logical_and(iota((16, LINES), 0) == 1, iota((16, LINES), 1) == 0),
             jnp.logical_and(iota((16, LINES), 0) == 8, iota((16, LINES), 1) == LINES - 1),
         )
-        sides = dot(edge_recv[t].reshape(16, NF), ones(spot), HIGHEST, ((0,), (0,)))
-        f = f_ref[...]
-        near = jnp.where(lane == 0, 0.0, pltpu.roll(f, 1, 1)) + jnp.where(
-            lane == LINES - 1, 0.0, pltpu.roll(f, LINES - 1, 1)
-        )
-        r_ref[...] = s_ref[...] + gain_col * (near + sides)
-
+        added = exact(ge[:, 0:NI].T, ones(spot), parts=2)
+        g_ref[...] = added
+
+    def add_edges():
+        r_ref[0:NI, :] = r_ref[0:NI, :] + dot3((xw_h[0:NI], xw_l[0:NI]), split(g_ref[...]))
+
+    def send_late(t):
+        for copy in late_copies(t):
+            copy.start()
+
+    def meet_stator(t):
+        f64_arrival(t).wait_recv()
+        h_ref[0:208, :] = jnp.zeros((208, LINES), F32)
+        h_ref[240:NI, :] = jnp.zeros((NI - 240, LINES), F32)
+        h_ref[208:216, :] = jnp.zeros((8, LINES), F32)
+        h_ref[210:245, :] = dot(c63_out[...], f64[t], HIGHEST)
+        both = dot3((xw_h[...], xw_l[...]), split(h_ref[...]))
+        late[t] = both[NI : NI + B]
+        send_late(t)
+        r_ref[0:NI, :] = r_ref[0:NI, :] + both[0:NI]
+
+    def collect(t, whose, dst):
+        lines = map_v[pl.ds(q if whose == 0 else q + 1 - 2 * core, 1), :]
+        for a in range(INST):
+            high, low_part = split(xin[a].reshape(zs * 8, LINES))
+            found = lax.rem(lines + slide_v[:, a : a + 1], pitches * LINES) // LINES
+            got = (dot(high, hot[whose, a]) + dot(low_part, hot[whose, a])).reshape(zs, 8, LINES)
+            which = 2 * iota((zs, 1, LINES), 0) + core == found.reshape(1, 1, LINES)
+            dst[VARS * a : VARS * a + VARS, :] = jnp.sum(jnp.where(which, got, 0.0), 0)[0:VARS]
+
+    def meet_rotor(t):
+        for copy in f63_arrivals(t):
+            copy.wait_recv()
+        for a in range(INST):
+            xin[a, :, 0:VARS, :] = f63[t, :, VARS * a : VARS * a + VARS, :]
+        collect(t, 1, pass_out.at[t])
+        pass_copy(t).start()
+        collect(t, 0, u_ref)
+        pass_copy(t).wait_recv()
+        late[t] = dot(c63[...], u_ref[0:B, :] + pass_in[t], HIGHEST)
+        send_late(t)
+
+    def interface(t):
         @pl.when(outlet)
         def _():
-            f64_arrival(t).wait_recv()
-            r_ref[210:245, :] = r_ref[210:245, :] + dot(c63_out[...], f64[t], HIGHEST)
-
-    def reach(t):
-        lines = map_v[pl.ds(q, 1), :]
-        total = [None] * INST
-        for half_at in range(2):
-            c = core if half_at == 0 else 1 - core
-            if half_at == 1:
-                forward_arrival(t).wait_recv()
-            for a in range(INST):
-                xin[a, :, 0:VARS, :] = f63[t, c, :, VARS * a : VARS * a + VARS, :]
-            for a in range(INST):
-                high, low_part = split(xin[a].reshape(zs * 8, LINES))
-                found = lax.rem(lines + slide_v[:, a : a + 1], pitches * LINES) // LINES
-                got = (dot(high, hot[a]) + dot(low_part, hot[a])).reshape(zs, 8, LINES)
-                which = 2 * iota((zs, 1, LINES), 0) + c == found.reshape(1, 1, LINES)
-                piece = jnp.sum(jnp.where(which, got, 0.0), 0)[0:VARS]
-                total[a] = piece if half_at == 0 else total[a] + piece
-        for a in range(INST):
-            u_ref[VARS * a : VARS * a + VARS, :] = total[a]
-        late[t] = dot(c63[...], u_ref[0:B, :], HIGHEST)
-        for copy in late_copies(t):
-            copy.start()
-
-    def send_sides(t):
-        rh, rl = split(r_ref[0:NI, :])
-        both = dot3((xw_h[...], xw_l[...]), (rh, rl))
-        r_ref[0:NI, :] = both[0:NI]
-        ends = both[NI:NF] + r_ref[NI:NF, :]
-        ab[t, l] = ends[0:72]
-        for copy in ab_copies(t):
-            copy.start()
+            meet_stator(t)
+
+        @pl.when(inlet)
+        def _():
+            meet_rotor(t)
 
     def finish(t):
-        for copy in ab_arrivals(t):
+        for copy in end_arrivals(t, *ends_of) + end_arrivals(t, *corrections):
             copy.wait_recv()
-        pb[0:B, :] = jnp.zeros((B, LINES), F32)
-        pa[B * CHAIN : NR, :] = jnp.zeros((NR - B * CHAIN, LINES), F32)
+        spread = exact(corr[t].reshape(8 * CHAIN, 128).T, spread_pick, parts=2)
         for s in range(CHAIN):
-            pa[B * s : B * s + B, :] = ab[t, s, 0:B, :]
-            pb[B * s + B : B * s + 2 * B, :] = ab[t, s, B : 2 * B, :]
+            piece = spread[:, LINES * s : LINES * s + LINES]
+            pa[B * s : B * s + B, :] = ab[t, s, 0:B, :] + piece[0:B]
+            pb[B * s + B : B * s + 2 * B, :] = ab[t, s, B : 2 * B, :] + piece[B : 2 * B]
+
+        @pl.when(jnp.logical_not(jnp.logical_or(inlet, outlet)))
+        def _():
+            late_arrival(t).wait_recv()
 
         @pl.when(stator)
         def _():
-            @pl.when(jnp.logical_not(inlet))
-            def _():
-                late_arrival(t).wait_recv()
-
             pa[0:B, :] = pa[0:B, :] + late[t]
+
+        @pl.when(jnp.logical_not(stator))
+        def _():
+            pa[B * (CHAIN - 1) : B * CHAIN, :] = pa[B * (CHAIN - 1) : B * CHAIN, :] + late[t]
 
         ends = dot3((yt_h[...], yt_l[...]), split(pa[...] + pb[0:NR, :]))
         if t == 0:
@@ -459,12 +499,17 @@
         f_ref[0:NI, :] = r_ref[0:NI, :] + dot3((w_h[...], w_l[...]), split(ends))
         f_ref[NI:NF, :] = ends
 
-    right_side(0)
-    send_sides(0)
-
-    @pl.when(inlet)
-    def _():
-        reach(0)
+    sides(0)
+    edges(0)
+    add_edges()
+    interface(0)
+    pb[0:B, :] = jnp.zeros((B, LINES), F32)
+    pa[B * CHAIN : NR, :] = jnp.zeros((NR - B * CHAIN, LINES), F32)
+    lines_at, pick_at = iota((8 * CHAIN, LINES * CHAIN), 1), iota((8 * CHAIN, LINES * CHAIN), 0)
+    spread_pick = ones(jnp.logical_or(
+        lines_at == LINES * (pick_at // 8) + jnp.where(lax.rem(pick_at, 8) == 1, 0, -1 - LINES * CHAIN),
+        lines_at == LINES * (pick_at // 8) + jnp.where(lax.rem(pick_at, 8) == 0, LINES - 1, -1 - LINES * CHAIN),
+    )).astype(BF16)
 
     for copy in kq_arrivals():
         copy.wait_recv()
@@ -481,9 +526,9 @@
     diag_tile = ones(jnp.logical_or(source_row == rcol_off, source_row == rcol_off + 128 + 2 * B))
     link_tile = ones(iota((128, NR), 0) == rcol_off + B)
     link_turn = ones(iota((NR, 128), 1) == rrow_off + B)
-    diag = dot(qq[...], diag_tile, HIGHEST)
-    above = dot(qq[:, 0:128], link_tile, HIGHEST)
-    below = dot(link_turn, qq[:, 0:128], HIGHEST, ((1,), (1,)))
+    diag = exact(qq[...], diag_tile)
+    above = exact(qq[:, 0:128], link_tile)
+    below = exact(qq[:, 0:128], link_turn, ((1,), (1,)), True)
     rotor_plan, stator_plan = plan(scalar_bounds(False), REDUCED_STEPS), plan(scalar_bounds(True), REDUCED_STEPS)
     mid, half_inv, first, scale = (
         jnp.where(stator, jnp.asarray(b, F32), jnp.asarray(a, F32))
@@ -510,11 +555,12 @@
     )
     wanted = jnp.where(want, col_scale, 0.0)
     yred[...] = xr
-    y = dot3(split(wanted), split(yred[...]))
-    for _ in range(2):
-        rest = wanted - dot(y, rmat[...], HIGHEST)
-        y += dot(rest.astype(BF16), yred[...].astype(BF16))
-    yt_h[...], yt_l[...] = split(y * col_scale)
+    few = wanted[0:80]
+    y = dot3(split(few), split(yred[...]))
+    y += dot((few - dot3(split(y), split(rmat[...]))).astype(BF16), yred[...].astype(BF16))
+    y += dot((few - dot(y, rmat[...], HIGHEST)).astype(BF16), yred[...].astype(BF16))
+    yt_h[80:128], yt_l[80:128] = jnp.zeros((48, NR), BF16), jnp.zeros((48, NR), BF16)
+    yt_h[0:80], yt_l[0:80] = split(y * col_scale)
 
     finish(0)
 
@@ -522,21 +568,17 @@
     send_outlet(1)
     place_edges(1)
     send_edges(1)
-    right_side(1)
-    send_sides(1)
-    forward(1)
-
-    @pl.when(inlet)
-    def _():
-        reach(1)
-
+    sides(1)
+    edges(1)
+    interface(1)
+    add_edges()
     finish(1)
     out_ref[pl.ds(0, B, stride=CELLS), :] = f_ref[NI : NI + B, :]
     for m in range(7):
         out_ref[pl.ds(m + 1, B, stride=CELLS), :] = f_ref[B * m : B * m + B, :]
 
     for t in range(2):
-        for copy in edge_copies(t) + tuple(ab_copies(t)):
+        for copy in list(edge_copies(t)) + end_copies(t, *ends_of) + end_copies(t, *corrections):
             copy.wait_send()
     for copy in kq_copies():
         copy.wait_send()
@@ -544,14 +586,14 @@
     @pl.when(outlet)
     def _():
         for t in range(2):
-            for copy in f63_copies(t):
+            for copy in f63_copies(t) + late_copies(t):
                 copy.wait_send()
         c63_copy(p + 1).wait_send()
 
     @pl.when(inlet)
     def _():
         for t in range(2):
-            forward_copy(t).wait_send()
+            pass_copy(t).wait_send()
             f64_copy(t).wait_send()
             for copy in late_copies(t):
                 copy.wait_send()
@@ -571,6 +613,7 @@
         out_specs=vmem,
         scratch_shapes=shapes + [
             V((NF, LINES), F32), V((NF, LINES), F32), V((NF, LINES), F32),
+            V((NI, LINES), F32), V((NI, LINES), F32),
             V((NI, B), F32), V((NI, B), F32),
             V((NI, NI), F32), V((NI, NI), F32), V((NI, NI), F32),
             V((4 * NR, NR), BF16), V((2 * NR, NR), BF16),
@@ -581,15 +624,16 @@
             V((128, NR), BF16), V((128, NR), BF16),
             V((NR, 256), F32),
             V((NR, LINES), F32), V((B * (CHAIN + 1) + 5, LINES), F32),
-            V((INST, LINES, LINES), BF16),
+            V((2, INST, LINES, LINES), BF16),
             V((INST, zs, 8, LINES), F32),
             V((2, 8, NF), F32), V((2, 2, 8, NF), F32),
             V((CHAIN, 40, 128), F32),
-            V((2, CHAIN, 72, LINES), F32),
-            V((2, 2, zs, B, LINES), F32), V((2, B, LINES), F32),
+            V((2, CHAIN, 72, LINES), F32), V((2, CHAIN, 8, 128), F32),
+            V((2, B, LINES), F32), V((2, B, LINES), F32),
+            V((2, zs, B, LINES), F32), V((2, B, LINES), F32),
             V((2, B, LINES), F32), V((2, B, LINES), F32),
             V((B, B), F32), V((B, B), F32), V((2, B, LINES), F32),
-            dma((CHAIN,)), dma((CHAIN,)), dma((2, CHAIN)), dma((2, CHAIN)),
+            dma((CHAIN,)), dma((CHAIN,)), dma((2, CHAIN)), dma((2, CHAIN)), dma((2, CHAIN)), dma((2, CHAIN)),
             dma((2, 2)), dma((2, 2)), dma((2, zs)), dma((2, zs)),
             dma((2,)), dma((2,)), dma((2,)), dma((2,)), dma, dma,
             dma((2, CHAIN)), dma((2,)), dma((7,)),

time: 43.5 us -> 41.2 us (0.947)
  the two profiles are of different devices: /device:TPU:5 before, /device:TPU:31 now
where the time goes in v3:
time: 41.2 us; the launch traced here: 41.1 us
  Pallas kernels  39.5 us (96%)
  local copies, waits for them, and re-layouts  1.58 us (4%)
    pallas_call x1, Pallas kernels, body(): pl.pallas_call(functools.partial(kernel, pitches), out_shape=jax.ShapeDty...  39.5 us
    unnamed x1, local copies, waits for them, and re-layouts  1.58 us

profile of v3, /device:TPU:31, one launch (start us, length us, event | category | flops | bytes accessed | tf_op | source)
XLA Modules:
  0.0 41.1 jit_solution(12047684044382595981)
XLA Ops:
  0.0 39.5 %sweeps.1 = f32[280,128]{1,0:T(8,128)} custom-call(f32[280,128]{1,0:T(8,128)} %bitcast.15, f32[280,128]{1,0:T(8,128)} %bitcast.16, f32[280,35]{1,0:T(8,128)} %bitcast.17, f32[8,35]{1,0:T(8,128)} %refs_3_.1, f32[8,35]{1,0:T(8,128)} %refs_4_.1, s32[16,128]{1,0:T(8,128)} %bitcast.18, s32[1,7]{1,0:T(1,128)} %bitcast.19), custom_call_target="tpu_custom_call" | custom-call | tf_op jit(solution)/shard_map/sweeps/pallas_call | solution.py:609
  39.5 1.6 %copy.9 = f32[8,35,128]{2,0,1:T(8,128)} copy(f32[8,35,128]{2,0,1:T(8,128)} %bitcast.14) | data formatting | bytes 286720

commit v4 on v3

--- a/solution.py
+++ b/solution.py
@@ -219,7 +219,6 @@
     place_edges(0)
     for i in (1, 3, 4, 5, 6):
         loads[i].wait()
-    pl.semaphore_wait(barrier, CHAIN + 1 + jnp.where(outlet, zs, 0) + jnp.where(inlet, 1, 0))
 
     def edge_copies(t):
         return (
@@ -303,14 +302,6 @@
 
     def late_arrival(t):
         return remote(late.at[t], late.at[t], late_s.at[t, 0], late_r.at[t], jnp.where(stator, CHAIN, CHAIN - 1), q)
-
-    send_outlet(0)
-    send_inlet(0)
-    send_edges(0)
-
-    @pl.when(outlet)
-    def _():
-        c63_copy(p + 1).start()
 
     stack(s_ref, source_v)
     pick_cell = ones(row_cell == iota((NF, CELLS), 1))
@@ -363,6 +354,15 @@
     links = links[:, 0:128]
     links += jnp.where(iota((NI, 128), 1) == row_off[0:NI] + 2 * B, g_in, 0.0)
     chebyshev(NI, jnp.asarray(first, F32), 1.0 / half, lhs, rhs, ymat, tmat, LOCAL_STEPS, True)
+    pl.semaphore_wait(barrier, CHAIN + 1 + jnp.where(outlet, zs, 0) + jnp.where(inlet, 1, 0))
+    send_outlet(0)
+    send_inlet(0)
+    send_edges(0)
+
+    @pl.when(outlet)
+    def _():
+        c63_copy(p + 1).start()
+
     x0 = ymat[...] * scale
     ymat[...] = x0
     rest = jnp.where(same, 1.0, 0.0) - dot(smat[...], ymat[...], HIGHEST)
@@ -394,6 +394,14 @@
     for copy in kq_copies():
         copy.start()
 
+    def send_ends(t):
+        for copy in end_copies(t, *ends_of):
+            copy.start()
+
+    def send_corrections(t):
+        for copy in end_copies(t, *corrections):
+            copy.start()
+
     def sides(t):
         f = f_ref[...]
         near = jnp.where(lane == 0, 0.0, pltpu.roll(f, 1, 1)) + jnp.where(
@@ -402,8 +410,8 @@
         r_ref[...] = s_ref[...] + gain_col * near
         both = dot3((xw_h[...], xw_l[...]), split(r_ref[0:NI, :]))
         ab[t, l] = (both[NI:NF] + r_ref[NI:NF, :])[0:72]
-        for copy in end_copies(t, *ends_of):
-            copy.start()
+        if t == 1:
+            send_ends(t)
         r_ref[0:NI, :] = both[0:NI]
 
     def edges(t):
@@ -414,8 +422,8 @@
         short = dot3((ge_h[:, 0:NI], ge_l[:, 0:NI]), (w_h[...], w_l[...])) + ge[:, NI:NF]
         which = iota((8, 128), 0)
         corr[t, l] = jnp.where(which == 1, short[0:8], 0.0) + jnp.where(which == 0, short[8:16], 0.0)
-        for copy in end_copies(t, *corrections):
-            copy.start()
+        if t == 1:
+            send_corrections(t)
         spot = jnp.logical_or(
             jnp.logical_and(iota((16, LINES), 0) == 1, iota((16, LINES), 1) == 0),
             jnp.logical_and(iota((16, LINES), 0) == 8, iota((16, LINES), 1) == LINES - 1),
@@ -496,13 +504,19 @@
         if t == 0:
             f64_out[1] = ends[0:B]
             send_inlet(1)
+
+            @pl.when(outlet)
+            def _():
+                h_ref[208:NI, :] = r_ref[208:NI, :] + dot3((w_h[208:NI], w_l[208:NI]), split(ends))
+                f63_out[1] = h_ref[210:245, :]
+
+            send_outlet(1)
         f_ref[0:NI, :] = r_ref[0:NI, :] + dot3((w_h[...], w_l[...]), split(ends))
         f_ref[NI:NF, :] = ends
 
     sides(0)
     edges(0)
     add_edges()
-    interface(0)
     pb[0:B, :] = jnp.zeros((B, LINES), F32)
     pa[B * CHAIN : NR, :] = jnp.zeros((NR - B * CHAIN, LINES), F32)
     lines_at, pick_at = iota((8 * CHAIN, LINES * CHAIN), 1), iota((8 * CHAIN, LINES * CHAIN), 0)
@@ -513,6 +527,9 @@
 
     for copy in kq_arrivals():
         copy.wait_recv()
+    send_ends(0)
+    send_corrections(0)
+    interface(0)
     qq[0:B, 128:256] = jnp.zeros((B, 128), F32)
     qq[B * CHAIN : NR, :] = jnp.zeros((NR - B * CHAIN, 256), F32)
     for s in range(CHAIN):
@@ -564,8 +581,6 @@
 
     finish(0)
 
-    f63_out[1] = f_ref[210:245, :]
-    send_outlet(1)
     place_edges(1)
     send_edges(1)
     sides(1)
@@ -639,14 +654,16 @@
             dma((2, CHAIN)), dma((2,)), dma((7,)),
         ],
         compiler_params=pltpu.CompilerParams(
-            collective_id=0, has_side_effects=True, vmem_limit_bytes=60 * 2**20
+            collective_id=0, has_side_effects=True, vmem_limit_bytes=48 * 2**20
         ),
         name="sweeps",
     )(
-        field.transpose(1, 0, 2).reshape(B * CELLS, LINES),
-        source.transpose(1, 0, 2).reshape(B * CELLS, LINES),
-        couple.transpose(1, 0, 2).reshape(B * CELLS, B),
-        shift, gain, row_map.reshape(pitches, LINES), slide.reshape(1, INST),
+        *(pltpu.with_memory_space_constraint(x, pltpu.HBM) for x in (
+            field.transpose(1, 0, 2).reshape(B * CELLS, LINES),
+            source.transpose(1, 0, 2).reshape(B * CELLS, LINES),
+            couple.transpose(1, 0, 2).reshape(B * CELLS, B),
+            shift, gain, row_map.reshape(pitches, LINES), slide.reshape(1, INST),
+        ))
     )
     return out.reshape(B, CELLS, LINES).transpose(1, 0, 2)
 

time: 41.2 us -> 38.8 us (0.942)
  Pallas kernels: 39.5 us -> 38 us
  local copies, waits for them, and re-layouts: 1.58 us -> 0.66 us
    pallas_call x1, Pallas kernels: 39.5 us -> 38 us  [body(): pl.pallas_call(functools.partial(kernel, pitches), out_shape=jax.ShapeDty...]
    unnamed x1, local copies, waits for them, and re-layouts: 1.58 us -> 0.66 us
where the time goes in v4:
time: 38.8 us; the launch traced here: 38.7 us
  Pallas kernels  38 us (98%)
  local copies, waits for them, and re-layouts  0.66 us (2%)
    pallas_call x1, Pallas kernels, body(): pl.pallas_call(functools.partial(kernel, pitches), out_shape=jax.ShapeDty...  38 us

profile of v4, /device:TPU:31, one launch (start us, length us, event | category | flops | bytes accessed | tf_op | source)
XLA Modules:
  0.0 38.7 jit_solution(10127312407347540761)
XLA Ops:
  0.0 38.0 %sweeps.1 = f32[280,128]{1,0:T(8,128)S(1)} custom-call(f32[280,128]{1,0:T(8,128)} %bitcast.15, f32[280,128]{1,0:T(8,128)} %bitcast.16, f32[280,35]{1,0:T(8,128)} %bitcast.17, f32[8,35]{1,0:T(8,128)} %refs_3_.1, f32[8,35]{1,0:T(8,128)} %refs_4_.1, s32[16,128]{1,0:T(8,128)} %bitcast.18, s32[1,7]{1,0:T(1,128)} %bitcast.19), custom_call_target="tpu_custom_call" | custom-call | tf_op jit(solution)/shard_map/sweeps/pallas_call | solution.py:624
  38.0 0.7 %copy.9 = f32[8,35,128]{2,0,1:T(8,128)} copy(f32[8,35,128]{2,0,1:T(8,128)S(1)} %bitcast.14) | data formatting | bytes 286720

commit v5 on v4

--- a/solution.py
+++ b/solution.py
@@ -91,8 +91,9 @@
 
 
 def chebyshev(n, t, half_inv, lhs, rhs, y_ref, t_ref, steps, exact):
+    m = min(n, 256)
+    rows = 4 if exact else 3
     eye = ones(iota((n, n), 0) == iota((n, n), 1))
-    rows = 4 if exact else 3
 
     def load(with_y):
         th, tl = split(t_ref[...])
@@ -105,31 +106,52 @@
         elif with_y:
             lhs[2 * n : 3 * n, 0:n] = y_ref[...].astype(BF16)
 
+    def corner(block, part):
+        if n == m:
+            return None
+        return dot(lhs[block * n + m : block * n + n, 0:n], rhs[part * n : part * n + n, m:n])
+
+    def times(first, last, part=0):
+        return dot(lhs[first * n : last * n, 0:n], rhs[part * n : part * n + n, 0:m])
+
+    def put(ref, update, main, rest):
+        value = update(ref[:, 0:m], main, eye[:, 0:m])
+        if n > m:
+            end = update(ref[m:n, m:n], rest, eye[0 : n - m, 0 : n - m])
+            ref[0:m, m:n] = value[m:n].T
+            ref[m:n, m:n] = end
+        ref[:, 0:m] = value
+
+    def squared(big):
+        main = big[0:n] + (big[n : 2 * n] + times(0, 1, 1))
+        return main, None if n == m else corner(0, 0) + (corner(1, 0) + corner(0, 1))
+
+    def turn(_, square, one):
+        return 2.0 * square - one
+
     load(False)
-    big = dot(lhs[0 : 2 * n, 0:n], rhs[0:n, 0:n])
-    square = big[0:n] + (big[n : 2 * n] + dot(lhs[0:n, 0:n], rhs[n : 2 * n, 0:n]))
+    square = squared(times(0, 2))
     y_ref[...] = (2.0 * half_inv) * (t * eye + t_ref[...])
-    t_ref[...] = 2.0 * square - eye
+    put(t_ref, turn, *square)
     t = 2.0 * t * t - 1.0
+
+    def grow(t, big):
+        mixed, rest = big[0:n], corner(2, 0)
+        if exact:
+            mixed = mixed + (big[n : 2 * n] + times(2, 3, 1))
+        put(y_ref, lambda y, product, _: 2.0 * (t * y + product), mixed, rest)
 
     def step(_, t):
         load(True)
-        big = dot(lhs[0 : rows * n, 0:n], rhs[0:n, 0:n])
-        square = big[0:n] + (big[n : 2 * n] + dot(lhs[0:n, 0:n], rhs[n : 2 * n, 0:n]))
-        mixed = big[2 * n : 3 * n]
-        if exact:
-            mixed += big[3 * n : 4 * n] + dot(lhs[2 * n : 3 * n, 0:n], rhs[n : 2 * n, 0:n])
-        t_ref[...] = 2.0 * square - eye
-        y_ref[...] = 2.0 * (t * y_ref[...] + mixed)
+        big = times(0, rows)
+        square = squared(big)
+        grow(t, big[2 * n :])
+        put(t_ref, turn, *square)
         return 2.0 * t * t - 1.0
 
     t = lax.fori_loop(0, steps - 2, step, t)
     load(True)
-    big = dot(lhs[2 * n : rows * n, 0:n], rhs[0:n, 0:n])
-    mixed = big[0:n]
-    if exact:
-        mixed += big[n : 2 * n] + dot(lhs[2 * n : 3 * n, 0:n], rhs[n : 2 * n, 0:n])
-    y_ref[...] = 2.0 * (t * y_ref[...] + mixed)
+    grow(t, times(2, rows))
 
 
 def kernel(
@@ -203,7 +225,6 @@
         dst[NI : NI + B, :] = cell_of(src, 0)
 
     loads[0].wait()
-    stack(f_ref, field_v)
     f63_out[0] = cell_of(field_v, CELLS - 1)
     f64_out[0] = cell_of(field_v, 0)
     loads[2].wait()
@@ -216,7 +237,6 @@
         )
         edge_send[t] = exact(f_ref[...], ones(pick), ((1,), (1,)), True, 2)
 
-    place_edges(0)
     for i in (1, 3, 4, 5, 6):
         loads[i].wait()
 
@@ -303,29 +323,11 @@
     def late_arrival(t):
         return remote(late.at[t], late.at[t], late_s.at[t, 0], late_r.at[t], jnp.where(stator, CHAIN, CHAIN - 1), q)
 
-    stack(s_ref, source_v)
     pick_cell = ones(row_cell == iota((NF, CELLS), 1))
     own = row_off == iota((NF, B), 1)
     gain_col = jnp.sum(jnp.where(own, dot(pick_cell, gain_v[...], HIGHEST), 0.0), 1, keepdims=True)
     shift_col = jnp.sum(jnp.where(own, dot(pick_cell, shift_v[...], HIGHEST), 0.0), 1, keepdims=True)
     g_col = shift_col + 2.0 * gain_col
-    place = iota((1, NF), 1)
-    place_block = jnp.where(place < 245, block_of(place, 7), 0)
-    place_sep = jnp.logical_and(place >= NI, place < NI + B)
-    place_off = jnp.where(place_sep, place - NI, place - B * place_block)
-    place_cell = jnp.where(place < 245, place_block + 1, jnp.where(place_sep, 0, -1))
-    gains = dot(gain_v[...], ones(place_cell == iota((CELLS, NF), 0)), HIGHEST, ((0,), (0,)))
-    gain_row = jnp.sum(jnp.where(place_off == iota((B, NF), 0), gains, 0.0), 0, keepdims=True)
-
-    @pl.when(inlet)
-    def _():
-        lines = map_v[pl.ds(q, 1), :]
-        xin[...] = jnp.zeros_like(xin)
-        other_lines = map_v[pl.ds(q + 1 - 2 * core, 1), :]
-        for whose, wanted_lines in enumerate((lines, other_lines)):
-            for a in range(INST):
-                found = lax.rem(wanted_lines + slide_v[:, a : a + 1], pitches * LINES)
-                hot[whose, a] = ones(iota((LINES, LINES), 0) == lax.rem(found, LINES)).astype(BF16)
 
     cl_ref[240:NI, :] = jnp.zeros((NI - 240, B), F32)
     cr_ref[240:NI, :] = jnp.zeros((NI - 240, B), F32)
@@ -357,7 +359,6 @@
     pl.semaphore_wait(barrier, CHAIN + 1 + jnp.where(outlet, zs, 0) + jnp.where(inlet, 1, 0))
     send_outlet(0)
     send_inlet(0)
-    send_edges(0)
 
     @pl.when(outlet)
     def _():
@@ -393,6 +394,29 @@
 
     for copy in kq_copies():
         copy.start()
+
+    stack(f_ref, field_v)
+    place_edges(0)
+    send_edges(0)
+    stack(s_ref, source_v)
+    place = iota((1, NF), 1)
+    place_block = jnp.where(place < 245, block_of(place, 7), 0)
+    place_sep = jnp.logical_and(place >= NI, place < NI + B)
+    place_off = jnp.where(place_sep, place - NI, place - B * place_block)
+    place_cell = jnp.where(place < 245, place_block + 1, jnp.where(place_sep, 0, -1))
+    gains = dot(gain_v[...], ones(place_cell == iota((CELLS, NF), 0)), HIGHEST, ((0,), (0,)))
+    gain_row = jnp.sum(jnp.where(place_off == iota((B, NF), 0), gains, 0.0), 0, keepdims=True)
+
+    @pl.when(inlet)
+    def _():
+        lines = map_v[pl.ds(q, 1), :]
+        xin[...] = jnp.zeros_like(xin)
+        other_lines = map_v[pl.ds(q + 1 - 2 * core, 1), :]
+        for whose, wanted_lines in enumerate((lines, other_lines)):
+            for a in range(INST):
+                found = lax.rem(wanted_lines + slide_v[:, a : a + 1], pitches * LINES)
+                hot[whose, a] = ones(iota((LINES, LINES), 0) == lax.rem(found, LINES)).astype(BF16)
+
 
     def send_ends(t):
         for copy in end_copies(t, *ends_of):
@@ -466,6 +490,8 @@
         collect(t, 1, pass_out.at[t])
         pass_copy(t).start()
         collect(t, 0, u_ref)
+
+    def meet_both(t):
         pass_copy(t).wait_recv()
         late[t] = dot(c63[...], u_ref[0:B, :] + pass_in[t], HIGHEST)
         send_late(t)
@@ -477,7 +503,9 @@
 
         @pl.when(inlet)
         def _():
-            meet_rotor(t)
+            if t == 1:
+                meet_rotor(t)
+            meet_both(t)
 
     def finish(t):
         for copy in end_arrivals(t, *ends_of) + end_arrivals(t, *corrections):
@@ -517,6 +545,11 @@
     sides(0)
     edges(0)
     add_edges()
+
+    @pl.when(inlet)
+    def _():
+        meet_rotor(0)
+
     pb[0:B, :] = jnp.zeros((B, LINES), F32)
     pa[B * CHAIN : NR, :] = jnp.zeros((NR - B * CHAIN, LINES), F32)
     lines_at, pick_at = iota((8 * CHAIN, LINES * CHAIN), 1), iota((8 * CHAIN, LINES * CHAIN), 0)

time: 38.8 us -> 37.6 us (0.969)
  Pallas kernels: 38 us -> 36.7 us
    pallas_call x1, Pallas kernels: 38 us -> 36.7 us  [body(): pl.pallas_call(functools.partial(kernel, pitches), out_shape=jax.ShapeDty...]
where the time goes in v5:
time: 37.6 us; the launch traced here: 37.3 us
  Pallas kernels  36.7 us (98%)
  local copies, waits for them, and re-layouts  0.66 us (2%)
    pallas_call x1, Pallas kernels, body(): pl.pallas_call(functools.partial(kernel, pitches), out_shape=jax.ShapeDty...  36.7 us

profile of v5, /device:TPU:31, one launch (start us, length us, event | category | flops | bytes accessed | tf_op | source)
XLA Modules:
  0.0 37.3 jit_solution(4696578218834915961)
XLA Ops:
  0.0 36.7 %sweeps.1 = f32[280,128]{1,0:T(8,128)S(1)} custom-call(f32[280,128]{1,0:T(8,128)} %bitcast.15, f32[280,128]{1,0:T(8,128)} %bitcast.16, f32[280,35]{1,0:T(8,128)} %bitcast.17, f32[8,35]{1,0:T(8,128)} %refs_3_.1, f32[8,35]{1,0:T(8,128)} %refs_4_.1, s32[16,128]{1,0:T(8,128)} %bitcast.18, s32[1,7]{1,0:T(1,128)} %bitcast.19), custom_call_target="tpu_custom_call" | custom-call | tf_op jit(solution)/shard_map/sweeps/pallas_call | solution.py:657
  36.7 0.7 %copy.9 = f32[8,35,128]{2,0,1:T(8,128)} copy(f32[8,35,128]{2,0,1:T(8,128)S(1)} %bitcast.14) | data formatting | bytes 286720

commit v6 on v5

--- a/solution.py
+++ b/solution.py
@@ -355,7 +355,6 @@
     links += jnp.where(jnp.logical_and(in_block == 6, col_block == 1), rep_r, 0.0)
     links = links[:, 0:128]
     links += jnp.where(iota((NI, 128), 1) == row_off[0:NI] + 2 * B, g_in, 0.0)
-    chebyshev(NI, jnp.asarray(first, F32), 1.0 / half, lhs, rhs, ymat, tmat, LOCAL_STEPS, True)
     pl.semaphore_wait(barrier, CHAIN + 1 + jnp.where(outlet, zs, 0) + jnp.where(inlet, 1, 0))
     send_outlet(0)
     send_inlet(0)
@@ -364,6 +363,7 @@
     def _():
         c63_copy(p + 1).start()
 
+    chebyshev(NI, jnp.asarray(first, F32), 1.0 / half, lhs, rhs, ymat, tmat, LOCAL_STEPS, True)
     x0 = ymat[...] * scale
     ymat[...] = x0
     rest = jnp.where(same, 1.0, 0.0) - dot(smat[...], ymat[...], HIGHEST)

time: 37.6 us -> 38.3 us (1.019)
  Pallas kernels: 36.7 us -> 37.3 us
    pallas_call x1, Pallas kernels: 36.7 us -> 37.3 us  [body(): pl.pallas_call(functools.partial(kernel, pitches), out_shape=jax.ShapeDty...]
where the time goes in v6:
time: 38.3 us; the launch traced here: 38 us
  Pallas kernels  37.3 us (97%)
  local copies, waits for them, and re-layouts  0.66 us (2%)
    pallas_call x1, Pallas kernels, body(): pl.pallas_call(functools.partial(kernel, pitches), out_shape=jax.ShapeDty...  37.3 us

profile of v6, /device:TPU:31, one launch (start us, length us, event | category | flops | bytes accessed | tf_op | source)
XLA Modules:
  0.0 38.0 jit_solution(8317322729955077427)
XLA Ops:
  0.0 37.3 %sweeps.1 = f32[280,128]{1,0:T(8,128)S(1)} custom-call(f32[280,128]{1,0:T(8,128)} %bitcast.15, f32[280,128]{1,0:T(8,128)} %bitcast.16, f32[280,35]{1,0:T(8,128)} %bitcast.17, f32[8,35]{1,0:T(8,128)} %refs_3_.1, f32[8,35]{1,0:T(8,128)} %refs_4_.1, s32[16,128]{1,0:T(8,128)} %bitcast.18, s32[1,7]{1,0:T(1,128)} %bitcast.19), custom_call_target="tpu_custom_call" | custom-call | tf_op jit(solution)/shard_map/sweeps/pallas_call | solution.py:657
  37.4 0.7 %copy.9 = f32[8,35,128]{2,0,1:T(8,128)} copy(f32[8,35,128]{2,0,1:T(8,128)S(1)} %bitcast.14) | data formatting | bytes 286720
